TPU v7x, 512 devices: a whole 4x8x8 slice. The times are simulated.
512 devices in a mesh: box: 128 (over z, y, x_hi), seg: 4 (over x_lo, core).
Axes of the slice: x: 4 (x_hi: 2, x_lo: 2; x = x_hi * 2 + x_lo), y: 8, z: 8, core: 2. Of those that a mesh axis runs over, the one named last changes fastest.
Arguments:
- density_zero: bfloat16 [65536, 64], P('box'), may hold values from 0.25 to 4
- offsets: int32 [256, 4], P('box'), may hold values from -4 to 4, as said below
- start_one: int32 [128, 4, 1024], P('box', 'seg'), may hold values from 0 to 511, as said below
- slot_one: int32 [128, 4, 1024], P('box', 'seg'), may hold values from 0 to 3
- end_one: int32 [128, 4, 1024], P('box', 'seg'), may hold values from 0 to 255
- weight_one: float32 [128, 4, 1024], P('box', 'seg'), may hold values from 0.25 to 4
- start_two: int32 [128, 4, 1024], P('box', 'seg'), may hold values from 0 to 511, as said below
- slot_two: int32 [128, 4, 1024], P('box', 'seg'), may hold values from 0 to 3
- end_two: int32 [128, 4, 1024], P('box', 'seg'), may hold values from 0 to 255
- weight_two: float32 [128, 4, 1024], P('box', 'seg'), may hold values from 0.25 to 4
Outputs:
- density_one: bfloat16 [65536, 64], P('box')
- density_two: bfloat16 [65536, 64], P('box')
Inputs may be any that keep to these rules, and one draw needn't show every extreme that they name: `offsets`: in each row, the 4 entries are distinct. `start_one`: for every [g, l], each of the 512 rows appears exactly 1024 // 512 times. `start_two`: for every [g, l], each of the 512 rows appears exactly 1024 // 512 times.
All inputs are finite; a program needn't handle non-finite values.
Results may differ from a plain program's by a relative error of at most 0.009.
Values may be sent and summed in bfloat16 or wider, within the bound.
No kernel may reach another device: no remote copies, remote signals or barrier semaphores. Data moves between devices by JAX's collectives and lax.ppermute only.
A program may use at most 64 MiB of HBM per device.

v0:
```python
import jax
import jax.numpy as jnp
from jax import lax
from jax.sharding import PartitionSpec as P

REACH = 2


def from_behind(block, axis, distance):
    devices = range(lax.axis_size(axis))
    route = [((i - distance) % len(devices), i) for i in devices]
    return lax.ppermute(block, axis, route)


def three_parts(values):
    high = values.astype(jnp.bfloat16)
    rest = values - high.astype(jnp.float32)
    middle = rest.astype(jnp.bfloat16)
    low = (rest - middle.astype(jnp.float32)).astype(jnp.bfloat16)
    return (high, middle, low)


def onehot_left(table, values):
    total = None
    for member in three_parts(values):
        term = lax.dot_general(
            table, member, (((0,), (0,)), ((), ())), preferred_element_type=jnp.float32
        )
        total = term if total is None else total + term
    return total


def segment_pushes(start, slot, end, weight, scaled, width_k, block):
    rows, cols = scaled.shape
    blocks_dev = rows // block
    count = start.shape[0]
    step = min(2048, count)
    turns = count // step
    columns = blocks_dev * width_k * block

    def one_piece(acc, index):
        pick = (start[:, None] == jnp.arange(rows, dtype=jnp.int32)[None, :]).astype(jnp.bfloat16)
        fetched = jnp.dot(pick, scaled, preferred_element_type=jnp.float32)
        carried = fetched * weight[:, None]
        target = start // block * (width_k * block) + slot * block + end
        place = (target[:, None] == jnp.arange(columns, dtype=jnp.int32)[None, :]).astype(
            jnp.bfloat16
        )
        return (acc + onehot_left(place, carried), None)

    total, unused = lax.scan(one_piece, jnp.zeros((columns, cols), jnp.float32), jnp.arange(turns))
    return total.reshape(blocks_dev, width_k, block, cols)


def place_blocks(pushes, offsets):
    blocks_dev, width_k = offsets.shape
    span = 2 * REACH + 1
    target = jnp.arange(blocks_dev, dtype=jnp.int32)[:, None] + offsets + REACH * blocks_dev
    placing = (
        target[:, :, None] == jnp.arange(span * blocks_dev, dtype=jnp.int32)[None, None, :]
    ).astype(jnp.float32)
    return (placing, jnp.einsum("jku,jkec->uec", placing, pushes, precision=lax.Precision.HIGHEST))


def push_lanes(density, totals, start, slot, end, weight, offsets):
    rows, cols = density.shape
    blocks_dev, width_k = offsets.shape
    block = rows // blocks_dev
    span = 2 * REACH + 1
    scaled = (density.astype(jnp.float32) / totals[:, None]).astype(jnp.bfloat16)
    pushes = segment_pushes(start, slot, end, weight, scaled, width_k, block)
    placing, stacked = place_blocks(pushes, offsets)
    stacked = stacked.reshape(span, -1, 128)
    summed = lax.psum(stacked, "seg")
    combined = summed[REACH]
    for delta in range(-REACH, REACH + 1):
        if delta != 0:
            combined = combined + from_behind(summed[delta + REACH], "box", delta)
    return combined.reshape(rows, cols).astype(jnp.bfloat16)


def body(
    density_zero,
    offsets,
    start_one,
    slot_one,
    end_one,
    weight_one,
    start_two,
    slot_two,
    end_two,
    weight_two,
):
    rows = density_zero.shape[0]
    days = ((start_one, slot_one, end_one, weight_one), (start_two, slot_two, end_two, weight_two))
    flat = [tuple((member.reshape(-1) for member in day)) for day in days]
    density = density_zero
    results = []
    partial_totals = jnp.stack(
        [jax.ops.segment_sum(day[3], day[0], num_segments=rows) for day in flat]
    )
    totals = lax.psum(partial_totals, "seg")
    for number in range(2):
        starts, slots, ends, weights = flat[number]
        density = push_lanes(density, totals[number], starts, slots, ends, weights, offsets)
        results.append(density)
    return (results[0], results[1])


def solution(mesh):
    placed = (
        P("box", None),
        P("box", None),
        P("box", "seg", None),
        P("box", "seg", None),
        P("box", "seg", None),
        P("box", "seg", None),
        P("box", "seg", None),
        P("box", "seg", None),
        P("box", "seg", None),
        P("box", "seg", None),
    )
    return jax.shard_map(
        body,
        mesh=mesh,
        in_specs=placed,
        out_specs=(P("box", None), P("box", None)),
        check_vma=False,
    )
```

profile of v0, /device:TPU:1, one launch (start us, length us, event | category | flops | bytes accessed | tf_op | source)
XLA Modules:
  0.0 211.3 jit_solution(17053488340971013685)
XLA Ops:
  7.9 7.8 %scatter_custom_fusion = f32[512]{0:T(512)S(1)} fusion(s32[1024]{0:T(1024)} %bitcast.73, f32[1024]{0:T(1024)} %bitcast.82, f32[]{:T(128)} %constant.47.clone.1), kind=kCustom, calls=%fused_computation.91 | custom fusion | flops 1024 | bytes 2560 | tf_op jit(solution)/shard_map/scatter-add | solution.py:100
  15.7 7.8 %scatter_custom_fusion.1 = f32[512]{0:T(512)S(1)} fusion(s32[1024]{0:T(1024)} %bitcast.77, f32[1024]{0:T(1024)} %bitcast.84, f32[]{:T(128)} %constant.47.clone.1), kind=kCustom, calls=%fused_computation.89 | custom fusion | flops 1024 | bytes 2560 | tf_op jit(solution)/shard_map/scatter-add | solution.py:100
  23.4 11.9 %psum.21 = f32[2,512]{1,0:T(2,128)S(1)} all-reduce(f32[2,512]{1,0:T(2,128)S(1)} %pad_maximum_fusion), channel_id=1, replica_groups=mesh['box'=128,'seg'=4] {'seg'}, use_global_device_ids=true, to_apply=%region_2.0 | all-reduce | flops 1024 | bytes 8192 | tf_op jit(solution)/shard_map/psum | solution.py:102
  36.7 1.5 fusion.19
  38.2 1.8 fusion.4
  40.0 1.6 fusion.12
  41.6 1.8 fusion.13
  46.2 50.1 %all-reduce.3.cloned.1.call-done = f32[5,256,128]{2,1,0:T(8,128)} async-done(((f32[5,256,128]{2,1,0:T(8,128)}), f32[5,256,128]{2,1,0:T(8,128)}) %all-reduce.3.cloned.1.call-update) | async-done | bytes 655376 | tf_op jit(solution)/shard_map/psum | solution.py:74
  97.4 7.5 %collective-permute-start = (f32[256,128]{1,0:T(8,128)S(1)}, f32[256,128]{1,0:T(8,128)S(1)}, u32[]{:S(2)}, u32[]{:S(2)}) collective-permute-start(f32[256,128]{1,0:T(8,128)S(1)} %get-tuple-element.48), channel_id=1, source_target_pairs={{8,0},{12,4},{16,8},{20,12},{24,16},{28,20},{32,24},{36,28},{40,32... | collective-permute-start | bytes 393224 | tf_op jit(solution)/shard_map/ppermute | solution.py:12
  105.0 1.9 collective-permute-start.3
  106.9 4.3 %collective-permute-start.2 = (f32[256,128]{1,0:T(8,128)S(1)}, f32[256,128]{1,0:T(8,128)S(1)}, u32[]{:S(2)}, u32[]{:S(2)}) collective-permute-start(f32[256,128]{1,0:T(8,128)S(1)} %get-tuple-element.50), channel_id=1, source_target_pairs={{508,0},{0,4},{4,8},{8,12},{12,16},{16,20},{20,24},{24,28},{28,32}... | collective-permute-start | bytes 393224 | tf_op jit(solution)/shard_map/ppermute | solution.py:12
  111.2 6.9 %collective-permute-start.1 = (f32[256,128]{1,0:T(8,128)S(1)}, f32[256,128]{1,0:T(8,128)S(1)}, u32[]{:S(2)}, u32[]{:S(2)}) collective-permute-start(f32[256,128]{1,0:T(8,128)S(1)} %get-tuple-element.51), channel_id=1, source_target_pairs={{4,0},{8,4},{12,8},{16,12},{20,16},{24,20},{28,24},{32,28},{36,32}... | collective-permute-start | bytes 393224 | tf_op jit(solution)/shard_map/ppermute | solution.py:12
  118.2 1.9 collective-permute-done.2
  120.1 2.2 %collective-permute-done.1 = f32[256,128]{1,0:T(8,128)S(1)} collective-permute-done((f32[256,128]{1,0:T(8,128)S(1)}, f32[256,128]{1,0:T(8,128)S(1)}, u32[]{:S(2)}, u32[]{:S(2)}) %collective-permute-start.1) | collective-permute-done | bytes 131104 | tf_op jit(solution)/shard_map/ppermute | solution.py:12
  124.0 1.8 fusion.1
  125.8 1.6 fusion.14
  127.4 1.8 fusion.15
  131.9 44.8 %all-reduce.5.cloned.1.call-done = f32[5,256,128]{2,1,0:T(8,128)} async-done(((f32[5,256,128]{2,1,0:T(8,128)}), f32[5,256,128]{2,1,0:T(8,128)}) %all-reduce.5.cloned.1.call-update) | async-done | bytes 655376 | tf_op jit(solution)/shard_map/psum | solution.py:74
  177.9 7.5 %collective-permute-start.4 = (f32[256,128]{1,0:T(8,128)S(1)}, f32[256,128]{1,0:T(8,128)S(1)}, u32[]{:S(2)}, u32[]{:S(2)}) collective-permute-start(f32[256,128]{1,0:T(8,128)S(1)} %get-tuple-element.36), channel_id=1, source_target_pairs={{8,0},{12,4},{16,8},{20,12},{24,16},{28,20},{32,24},{36,28},{40,32... | collective-permute-start | bytes 393224 | tf_op jit(solution)/shard_map/ppermute | solution.py:12
  185.4 1.9 collective-permute-start.7
  187.3 4.3 %collective-permute-start.6 = (f32[256,128]{1,0:T(8,128)S(1)}, f32[256,128]{1,0:T(8,128)S(1)}, u32[]{:S(2)}, u32[]{:S(2)}) collective-permute-start(f32[256,128]{1,0:T(8,128)S(1)} %get-tuple-element.38), channel_id=1, source_target_pairs={{508,0},{0,4},{4,8},{8,12},{12,16},{16,20},{20,24},{24,28},{28,32}... | collective-permute-start | bytes 393224 | tf_op jit(solution)/shard_map/ppermute | solution.py:12
  191.7 6.7 %collective-permute-start.5 = (f32[256,128]{1,0:T(8,128)S(1)}, f32[256,128]{1,0:T(8,128)S(1)}, u32[]{:S(2)}, u32[]{:S(2)}) collective-permute-start(f32[256,128]{1,0:T(8,128)S(1)} %get-tuple-element.39), channel_id=1, source_target_pairs={{4,0},{8,4},{12,8},{16,12},{20,16},{24,20},{28,24},{32,28},{36,32}... | collective-permute-start | bytes 393224 | tf_op jit(solution)/shard_map/ppermute | solution.py:12
  199.1 1.4 collective-permute-done.6
  200.5 2.2 %collective-permute-done.5 = f32[256,128]{1,0:T(8,128)S(1)} collective-permute-done((f32[256,128]{1,0:T(8,128)S(1)}, f32[256,128]{1,0:T(8,128)S(1)}, u32[]{:S(2)}, u32[]{:S(2)}) %collective-permute-start.5) | collective-permute-done | bytes 131104 | tf_op jit(solution)/shard_map/ppermute | solution.py:12
  (40 shorter events, 14.1 us)
Async XLA Ops:
  7.2 89.1 %all-reduce.3.cloned.1.call-start = ((), (), s32[]{:S(2)}) async-start(), calls=%async_computation | async-start | bytes 1310720 | tf_op jit(solution)/shard_map/psum | solution.py:74
  45.0 1.2 copy-start
  46.1 72.0 %copy-start.1 = (s32[1,1,1024]{2,1,0:T(1,128)S(1)}, s32[1,1,1024]{2,1,0:T(1,128)}, u32[]{:S(2)}) copy-start(s32[1,1,1024]{2,1,0:T(1,128)} %param.18) | copy-start | bytes 12292
  46.1 72.0 %copy-start.2 = (s32[1,1,1024]{2,1,0:T(1,128)S(1)}, s32[1,1,1024]{2,1,0:T(1,128)}, u32[]{:S(2)}) copy-start(s32[1,1,1024]{2,1,0:T(1,128)} %param.16) | copy-start | bytes 12292
  46.1 77.2 %copy-start.3 = (f32[1,1,1024]{2,1,0:T(1,128)S(1)}, f32[1,1,1024]{2,1,0:T(1,128)}, u32[]{:S(2)}) copy-start(f32[1,1,1024]{2,1,0:T(1,128)} %param.19) | copy-start | bytes 12292
  46.1 130.6 %all-reduce.5.cloned.1.call-start = ((), (), s32[]{:S(2)}) async-start(), calls=%async_computation.1 | async-start | bytes 1310720 | tf_op jit(solution)/shard_map/psum | solution.py:74
  97.4 20.7 %collective-permute-start = (f32[256,128]{1,0:T(8,128)S(1)}, f32[256,128]{1,0:T(8,128)S(1)}, u32[]{:S(2)}, u32[]{:S(2)}) collective-permute-start(f32[256,128]{1,0:T(8,128)S(1)} %get-tuple-element.48), channel_id=1, source_target_pairs={{8,0},{12,4},{16,8},{20,12},{24,16},{28,20},{32,24},{36,28},{40,32... | collective-permute-start | bytes 393224 | tf_op jit(solution)/shard_map/ppermute | solution.py:12
  105.0 13.2 %collective-permute-start.3 = (f32[256,128]{1,0:T(8,128)S(1)}, f32[256,128]{1,0:T(8,128)S(1)}, u32[]{:S(2)}, u32[]{:S(2)}) collective-permute-start(f32[256,128]{1,0:T(8,128)S(1)} %get-tuple-element.49), channel_id=1, source_target_pairs={{504,0},{508,4},{0,8},{4,12},{8,16},{12,20},{16,24},{20,28},{24,32... | collective-permute-start | bytes 393224 | tf_op jit(solution)/shard_map/ppermute | solution.py:12
  106.9 13.2 %collective-permute-start.2 = (f32[256,128]{1,0:T(8,128)S(1)}, f32[256,128]{1,0:T(8,128)S(1)}, u32[]{:S(2)}, u32[]{:S(2)}) collective-permute-start(f32[256,128]{1,0:T(8,128)S(1)} %get-tuple-element.50), channel_id=1, source_target_pairs={{508,0},{0,4},{4,8},{8,12},{12,16},{16,20},{20,24},{24,28},{28,32}... | collective-permute-start | bytes 393224 | tf_op jit(solution)/shard_map/ppermute | solution.py:12
  111.2 11.0 %collective-permute-start.1 = (f32[256,128]{1,0:T(8,128)S(1)}, f32[256,128]{1,0:T(8,128)S(1)}, u32[]{:S(2)}, u32[]{:S(2)}) collective-permute-start(f32[256,128]{1,0:T(8,128)S(1)} %get-tuple-element.51), channel_id=1, source_target_pairs={{4,0},{8,4},{12,8},{16,12},{20,16},{24,20},{28,24},{32,28},{36,32}... | collective-permute-start | bytes 393224 | tf_op jit(solution)/shard_map/ppermute | solution.py:12
  177.9 21.2 %collective-permute-start.4 = (f32[256,128]{1,0:T(8,128)S(1)}, f32[256,128]{1,0:T(8,128)S(1)}, u32[]{:S(2)}, u32[]{:S(2)}) collective-permute-start(f32[256,128]{1,0:T(8,128)S(1)} %get-tuple-element.36), channel_id=1, source_target_pairs={{8,0},{12,4},{16,8},{20,12},{24,16},{28,20},{32,24},{36,28},{40,32... | collective-permute-start | bytes 393224 | tf_op jit(solution)/shard_map/ppermute | solution.py:12
  185.4 13.7 %collective-permute-start.7 = (f32[256,128]{1,0:T(8,128)S(1)}, f32[256,128]{1,0:T(8,128)S(1)}, u32[]{:S(2)}, u32[]{:S(2)}) collective-permute-start(f32[256,128]{1,0:T(8,128)S(1)} %get-tuple-element.37), channel_id=1, source_target_pairs={{504,0},{508,4},{0,8},{4,12},{8,16},{12,20},{16,24},{20,28},{24,32... | collective-permute-start | bytes 393224 | tf_op jit(solution)/shard_map/ppermute | solution.py:12
  187.3 13.2 %collective-permute-start.6 = (f32[256,128]{1,0:T(8,128)S(1)}, f32[256,128]{1,0:T(8,128)S(1)}, u32[]{:S(2)}, u32[]{:S(2)}) collective-permute-start(f32[256,128]{1,0:T(8,128)S(1)} %get-tuple-element.38), channel_id=1, source_target_pairs={{508,0},{0,4},{4,8},{8,12},{12,16},{16,20},{20,24},{24,28},{28,32}... | collective-permute-start | bytes 393224 | tf_op jit(solution)/shard_map/ppermute | solution.py:12
  191.7 11.0 %collective-permute-start.5 = (f32[256,128]{1,0:T(8,128)S(1)}, f32[256,128]{1,0:T(8,128)S(1)}, u32[]{:S(2)}, u32[]{:S(2)}) collective-permute-start(f32[256,128]{1,0:T(8,128)S(1)} %get-tuple-element.39), channel_id=1, source_target_pairs={{4,0},{8,4},{12,8},{16,12},{20,16},{24,20},{28,24},{32,28},{36,32}... | collective-permute-start | bytes 393224 | tf_op jit(solution)/shard_map/ppermute | solution.py:12
Sparse Core Ops, SparseCore 0:
  46.2 50.0 all-reduce.2
  132.0 44.6 all-reduce.4
where the time goes:
time: 212 us; the launch traced here: 211 us
  waiting for transfers between devices  103 us (49%)
  starting transfers between devices  41.2 us (19%)
  other arithmetic  19.5 us (9%)
  between operations  14.3 us (7%)
  matrix products  13.9 us (7%)
  blocking collectives  11.9 us (6%)
  local copies, waits for them, and re-layouts  7.8 us (4%)
    psum x2, waiting for transfers between devices, push_lanes(): summed = lax.psum(stacked, 'seg')  95 us
    ppermute x8, starting transfers between devices, from_behind(): return lax.ppermute(block, axis, route)  41.1 us
    scatter-add x2, other arithmetic, body(): jax.ops.segment_sum(day[3], day[0], num_segments=rows)  15.5 us
    psum x1, blocking collectives, body(): totals = lax.psum(partial_totals, 'seg')  11.9 us
    dot_general x6, matrix products, onehot_left(): lax.dot_general(table, member, (((0,), (0,)), ((), ())), preferred_elemen...  10.3 us
    ppermute x8, waiting for transfers between devices, from_behind(): return lax.ppermute(block, axis, route)  7.71 us
  transfers between devices with their start and end apart: 10, of which 6 were waited for; matrix products, arithmetic and copies ran while one was open for 0% of the time, Pallas kernels for 0%

commit v1 on v0

v1 whole, which is shorter than its diff:
```python
import functools

import jax
import jax.numpy as jnp
from jax import lax
from jax.experimental import pallas as pl
from jax.experimental.pallas import tpu as pltpu
from jax.sharding import PartitionSpec as P

F32 = jnp.float32
BF16 = jnp.bfloat16
BLOCK = 256
COLS = 64
WIDTH = 4
AXES = ("box", "seg")


def place():
    box = lax.axis_index("box")
    core = lax.axis_index("seg") % 2
    pair = box // 2
    return pair, box % 2, core, 1 - (pair + core) % 2


def pair_groups(boxes):
    pairs = boxes // 2
    groups = []
    for first in range(pairs):
        second = (first + 1) % pairs
        for chip in range(4):
            core = first % 2
            groups.append([first * 8 + chip * 2 + core, second * 8 + chip * 2 + core])
    return groups


def core_groups(boxes):
    return [[2 * chip, 2 * chip + 1] for chip in range(boxes * 2)]


def half_groups(boxes):
    groups = []
    for pair in range(boxes // 2):
        for core in range(2):
            groups.append([pair * 8 + 2 + core, pair * 8 + 4 + core])
            groups.append([pair * 8 + core, pair * 8 + 6 + core])
    return groups


def iota(shape, dim):
    return lax.broadcasted_iota(jnp.int32, shape, dim)


def sort_kernel(*refs):
    *ins, out_ref, pick_ref = refs
    rows = out_ref.shape[1]
    count = ins[0].shape[-1]
    step = 64
    lane = iota((step, count), 1).astype(F32)
    for day in range(2):
        start, slot, end, weight = (ref[0] for ref in ins[4 * day : 4 * day + 4])
        for at in range(0, rows, step):
            hit = start == iota((step, count), 0) + at
            first = jnp.min(jnp.where(hit, lane, float(count)), axis=1, keepdims=True)
            last = jnp.max(jnp.where(hit, lane, -1.0), axis=1, keepdims=True)
            pick_ref[at : at + step, :] = jnp.where(lane == first, 1.0, 0.0).astype(BF16)
            pick_ref[rows + at : rows + at + step, :] = jnp.where(lane == last, 1.0, 0.0).astype(BF16)
        high = weight.astype(BF16).astype(F32)
        middle = (weight - high).astype(BF16).astype(F32)
        low = weight - high - middle
        zero = jnp.zeros_like(weight)
        load = jnp.concatenate(
            [end.astype(F32), slot.astype(F32), high, middle, low, zero, zero, zero], axis=0
        ).astype(BF16)
        got = lax.dot_general(
            load, pick_ref[...], (((1,), (1,)), ((), ())), preferred_element_type=F32
        )
        target = got[1:2] * float(BLOCK) + got[0:1]
        total = got[2:3] + got[3:4] + got[4:5]
        out_ref[4 * day : 4 * day + 4, :] = jnp.concatenate(
            [target[:, :rows], target[:, rows:], total[:, :rows], total[:, rows:]], axis=0
        )


def counts_block(keys, weights, counts_ref):
    step = 32
    width = counts_ref.shape[1]
    for at in range(0, BLOCK, step):
        ends = (iota((step, width), 0) + at).astype(F32)
        total = None
        for key, weight in zip(keys, weights):
            term = jnp.where(key == ends, weight, 0.0)
            total = term if total is None else total + term
        counts_ref[at : at + step, :] = total.astype(BF16)


def first_kernel(lists_ref, density_ref, offsets_ref, side_ref, own_ref, meta_ref, key_ref, weight_ref, spread_ref, counts_ref, sums_ref):
    pair, half, core, ahead = place()
    lanes = lists_ref.shape[0]
    rows = lists_ref.shape[2]
    for day in range(2):
        keys = jnp.concatenate([lists_ref[lane, 4 * day : 4 * day + 2, :] for lane in range(lanes)], axis=0)
        weights = jnp.concatenate([lists_ref[lane, 4 * day + 2 : 4 * day + 4, :] for lane in range(lanes)], axis=0)
        weights = weights / jnp.sum(weights, axis=0, keepdims=True)
        if day == 0:
            key_ref[...] = keys
            weight_ref[...] = weights
        else:
            slots = jnp.floor(keys * (1.0 / BLOCK))
            ends = keys - slots * float(BLOCK)
            offs = jnp.concatenate(
                [jnp.full((1, 128), offsets_ref[j, s].astype(F32), F32) for j in range(2) for s in range(WIDTH)], axis=0
            )
            for part in range(rows // 128):
                cut = slice(128 * part, 128 * part + 128)
                meta_ref[32 * part : 32 * part + 32, :] = jnp.concatenate(
                    [ends[:, cut], slots[:, cut], weights[:, cut], offs], axis=0
                ).astype(BF16)
    zero = jnp.zeros((BLOCK, COLS), BF16)
    for j in range(2):
        block = density_ref[BLOCK * j : BLOCK * j + BLOCK, :]
        spread_ref[j, 0] = jnp.concatenate([block, zero], axis=1)
        spread_ref[j, 1] = jnp.concatenate([zero, block], axis=1)
    sums_ref[...] = jnp.zeros_like(sums_ref)
    for j in range(2):

        @pl.loop(0, WIDTH)
        def _(s):
            block = 2 * half + j + offsets_ref[j, s]
            where = jnp.where(block < 0, 0, jnp.where(block >= 4, 1, 2))
            inside = where == 2
            mine = jnp.logical_or(where == ahead, jnp.logical_and(inside, core == j))

            @pl.when(mine)
            def _():
                cut = slice(BLOCK * j, BLOCK * j + BLOCK)
                base = (s * BLOCK).astype(F32)
                keys = [key_ref[k : k + 1, cut] - base for k in range(2 * lanes)]
                weights = [weight_ref[k : k + 1, cut] for k in range(2 * lanes)]
                counts_block(keys, weights, counts_ref)
                spot = block & 3
                pushed = jnp.dot(counts_ref[...], spread_ref[j, spot >> 1], preferred_element_type=F32)
                at = jnp.where(inside, 1, 0)
                sums_ref[at, spot & 1] += pushed

    for part in range(2):
        cut = slice(BLOCK * part, BLOCK * part + BLOCK)
        side_ref[cut, :] = sums_ref[0, part].astype(BF16)
        own_ref[cut, :] = sums_ref[1, part]


def second_kernel(parts_ref, density_ref, side_ref, own_ref, spread_ref, counts_ref, sums_ref):
    pair, half, core, ahead = place()
    rows = 2 * BLOCK
    total = parts_ref[0, :rows, :].astype(F32) + parts_ref[1, :rows, :].astype(F32)
    total = total.astype(BF16).astype(F32)
    density_ref[...] = jnp.where(half == 0, total[:, :COLS], total[:, COLS:]).astype(BF16)
    left = iota((BLOCK, 128), 1) < COLS
    for j in range(4):
        block = total[BLOCK * (j & 1) : BLOCK * (j & 1) + BLOCK, :]
        kept = jnp.where(left if j < 2 else jnp.logical_not(left), block, 0.0)
        turned = pltpu.roll(kept, COLS, 1)
        spread_ref[j, j >> 1] = kept.astype(BF16)
        spread_ref[j, 1 - (j >> 1)] = turned.astype(BF16)
    sums_ref[...] = jnp.zeros_like(sums_ref)
    for j in range(4):
        group = j >> 1
        at = rows + 64 * (j & 1)
        lists = [parts_ref[group, at + 32 * q : at + 32 * q + 32, :].astype(F32) for q in range(2)]
        for s in range(WIDTH):
            offset = lists[0][24 + 4 * (j & 1) + s, 0].astype(jnp.int32)
            block = j + offset
            where = jnp.where(block < 0, 0, jnp.where(block >= 4, 1, 2))
            inside = where == 2
            mine = jnp.logical_or(where == ahead, jnp.logical_and(inside, core == (j & 1)))
            mine = jnp.logical_and(mine, ((block >> 1) & 1) == half)

            @pl.when(mine)
            def _():
                keys, weights = [], []
                for k in range(8):
                    pieces = [
                        (one[k : k + 1, :] - jnp.where(one[8 + k : 9 + k, :] == float(s), 0.0, 512.0), one[16 + k : 17 + k, :])
                        for one in lists
                    ]
                    keys.append(jnp.concatenate([piece[0] for piece in pieces], axis=1))
                    weights.append(jnp.concatenate([piece[1] for piece in pieces], axis=1))
                counts_block(keys, weights, counts_ref)
                pushed = jnp.dot(counts_ref[...], spread_ref[j, block & 1], preferred_element_type=F32)
                sums_ref[jnp.where(inside, 1, 0)] += pushed

    side_ref[...] = sums_ref[0].astype(BF16)
    own_ref[...] = sums_ref[1]


VMEM = pl.BlockSpec(memory_space=pltpu.VMEM)
SMEM = pl.BlockSpec(memory_space=pltpu.SMEM)


def call(kernel, name, ins, outs, scratch):
    return pl.pallas_call(
        kernel,
        out_shape=outs,
        in_specs=ins,
        out_specs=jax.tree.map(lambda _: VMEM, outs),
        scratch_shapes=scratch,
        compiler_params=pltpu.CompilerParams(vmem_limit_bytes=32 * 1024 * 1024),
        name=name,
    )


def body(density, offsets, *segments):
    boxes = lax.axis_size("box")
    rows = density.shape[0]
    count = segments[0].shape[-1]
    gather = functools.partial(lax.all_gather, axis_name=AXES)
    pair, half, core, ahead = place()

    lists = call(
        sort_kernel,
        "sort",
        [VMEM] * 8,
        jax.ShapeDtypeStruct((8, rows), F32),
        [pltpu.VMEM((2 * rows, count), BF16)],
    )(*[member.reshape(1, 1, count) for member in segments])
    lists = lax.all_gather(lists, "seg")
    side, own, meta = call(
        first_kernel,
        "first",
        [VMEM, VMEM, SMEM],
        (
            jax.ShapeDtypeStruct((rows, 128), BF16),
            jax.ShapeDtypeStruct((rows, 128), F32),
            jax.ShapeDtypeStruct((128, 128), BF16),
        ),
        [
            pltpu.VMEM((8, rows), F32),
            pltpu.VMEM((8, rows), F32),
            pltpu.VMEM((2, 2, BLOCK, 128), BF16),
            pltpu.VMEM((BLOCK, BLOCK), BF16),
            pltpu.VMEM((2, 2, BLOCK, 128), F32),
        ],
    )(lists, density, offsets)
    sides = gather(side, axis_index_groups=pair_groups(boxes))
    came = jnp.where(ahead == 1, sides[1], sides[0])
    mixed = (own + came.astype(F32)).astype(BF16)
    both = gather(mixed, axis_index_groups=core_groups(boxes))
    summed = (both[0].astype(F32) + both[1].astype(F32)).astype(BF16)
    parts = gather(jnp.concatenate([summed, meta], axis=0), axis_index_groups=half_groups(boxes))
    density_one, side, own = call(
        second_kernel,
        "second",
        [VMEM],
        (
            jax.ShapeDtypeStruct((rows, COLS), BF16),
            jax.ShapeDtypeStruct((BLOCK, 128), BF16),
            jax.ShapeDtypeStruct((BLOCK, 128), F32),
        ),
        [
            pltpu.VMEM((4, 2, BLOCK, 128), BF16),
            pltpu.VMEM((BLOCK, BLOCK), BF16),
            pltpu.VMEM((2, BLOCK, 128), F32),
        ],
    )(parts)
    sides = gather(side, axis_index_groups=pair_groups(boxes))
    came = jnp.where(ahead == 1, sides[1], sides[0])
    both = gather(own + came.astype(F32), axis_index_groups=core_groups(boxes))
    summed = (both[0] + both[1]).astype(BF16)
    density_two = jnp.concatenate([summed[:, :COLS], summed[:, COLS:]], axis=0)
    return density_one, density_two


def solution(mesh):
    boxed = P("box", None)
    lined = P("box", "seg", None)
    return jax.shard_map(
        body,
        mesh=mesh,
        in_specs=(boxed, boxed) + (lined,) * 8,
        out_specs=(boxed, boxed),
        check_vma=False,
    )
```

time: 212 us -> 51.5 us (0.24)
  waiting for transfers between devices: 103 us -> 0 us
  starting transfers between devices: 41.2 us -> 0 us
  blocking collectives: 11.9 us -> 39.6 us
  other arithmetic: 19.5 us -> 0.17 us
  matrix products: 13.9 us -> 0 us
  between operations: 14.3 us -> 0.81 us
  Pallas kernels: 0 us -> 7.79 us
  local copies, waits for them, and re-layouts: 7.8 us -> 2.93 us
    psum x2 -> x0, waiting for transfers between devices: 95 us -> none  [push_lanes(): summed = lax.psum(stacked, 'seg')]
    ppermute x8 -> x0, starting transfers between devices: 41.1 us -> none  [from_behind(): return lax.ppermute(block, axis, route)]
    all_gather x0 -> x6, blocking collectives: none -> 39.6 us  [the longest x2 15.4 us: body(): sides = gather(side, axis_index_groups=pair_groups(boxes))]
    scatter-add x2 -> x0, other arithmetic: 15.5 us -> none  [body(): jax.ops.segment_sum(day[3], day[0], num_segments=rows)]
    dot_general x10 -> x0, matrix products: 13.9 us -> none  [the longest x6 10.3 us: onehot_left(): lax.dot_general(table, member, (((0,), (0,)), ((), ())), preferred_elemen...]
    psum x1 -> x0, blocking collectives: 11.9 us -> none  [body(): totals = lax.psum(partial_totals, 'seg')]
    pallas_call x0 -> x3, Pallas kernels: none -> 7.79 us  [the longest x1 3.06 us: body(): call(first_kernel, 'first', [VMEM, VMEM, SMEM], (jax.ShapeDtypeStruct((ro...]
    ppermute x8 -> x0, waiting for transfers between devices: 7.71 us -> none  [from_behind(): return lax.ppermute(block, axis, route)]
  transfers between devices with their start and end apart: 10 -> 0, of which waited for: 6 -> 0; matrix products, arithmetic and copies ran while one was open for 0% -> 0% of each run, Pallas kernels for 0% -> 0%
where the time goes in v1:
time: 51.5 us; the launch traced here: 51.3 us
  blocking collectives  39.6 us (77%)
  Pallas kernels  7.79 us (15%)
  local copies, waits for them, and re-layouts  2.93 us (6%)
  between operations  0.81 us (2%)
    all_gather x2, blocking collectives, body(): sides = gather(side, axis_index_groups=pair_groups(boxes))  15.4 us
    all_gather x1, blocking collectives, body(): lists = lax.all_gather(lists, 'seg')  12 us
    all_gather x1, blocking collectives, body(): gather(jnp.concatenate([summed, meta], axis=0), axis_index_groups=half_gr...  8.22 us
    pallas_call x1, Pallas kernels, body(): call(first_kernel, 'first', [VMEM, VMEM, SMEM], (jax.ShapeDtypeStruct((ro...  3.06 us
    pallas_call x1, Pallas kernels, body(): call(second_kernel, 'second', [VMEM], (jax.ShapeDtypeStruct((rows, COLS),...  2.93 us
    unnamed x23, local copies, waits for them, and re-layouts  2.84 us
    all_gather x1, blocking collectives, body(): both = gather(mixed, axis_index_groups=core_groups(boxes))  1.99 us
    all_gather x1, blocking collectives, body(): both = gather(own + came.astype(F32), axis_index_groups=core_groups(boxes))  1.99 us

profile of v1, /device:TPU:1, one launch (start us, length us, event | category | flops | bytes accessed | tf_op | source)
XLA Modules:
  0.0 51.3 jit_solution(5994695820867461618)
XLA Ops:
  0.6 0.0 copy-start.7
  0.7 0.0 copy-start.5
  0.8 0.6 %copy-done.7 = f32[1,1,1024]{2,1,0:T(1,128)S(1)} copy-done((f32[1,1,1024]{2,1,0:T(1,128)S(1)}, f32[1,1,1024]{2,1,0:T(1,128)}, u32[]{:S(2)}) %copy-start.7) | copy-done | bytes 4120
  1.3 0.0 copy-done.6
  1.4 0.0 copy-done.5
  1.4 0.0 copy-done.4
  1.4 0.0 copy-done.3
  1.4 0.0 copy-done.2
  1.4 0.0 copy-done.1
  1.4 0.0 copy-done
  1.4 1.8 %sort.1 = f32[8,512]{1,0:T(8,128)S(1)} custom-call(s32[1,1,1024]{2,1,0:T(1,128)S(1)} %copy-done, s32[1,1,1024]{2,1,0:T(1,128)S(1)} %copy-done.1, s32[1,1,1024]{2,1,0:T(1,128)S(1)} %copy-done.2, f32[1,1,1024]{2,1,0:T(1,128)S(1)} %copy-done.3, s32[1,1,1024]{2,1,0:T(1,128)S(1)} %copy-done.4, s32[1,1,1024]{2,1,0:T(1,128)S(1)} %copy-done.5, ...), custom_call_target="tpu_custom_call" | custom-call | tf_op jit(solution)/shard_map/sort/pallas_call | solution.py:218
  3.3 12.0 %all-gather = f32[32,512]{1,0:T(8,128)S(1)} all-gather(f32[8,512]{1,0:T(8,128)S(1)} %sort.1), channel_id=2, replica_groups=mesh['box'=128,'seg'=4] {'seg'}, dimensions={0}, use_global_device_ids=true | all-gather | bytes 81920 | tf_op jit(solution)/shard_map/all_gather | solution.py:225
  15.2 0.1 copy.12.density_ref
  15.3 0.6 %copy-done.8 = s32[2,4]{1,0:T(2,128)S(1)} copy-done((s32[2,4]{1,0:T(2,128)S(1)}, s32[2,4]{1,0:T(2,128)}, u32[]{:S(2)}) %copy-start.8) | copy-done | bytes 56
  15.9 3.1 %first.1 = (bf16[512,128]{1,0:T(8,128)(2,1)S(1)}, f32[512,128]{1,0:T(8,128)S(1)}, bf16[128,128]{1,0:T(8,128)(2,1)S(1)}) custom-call(f32[4,8,512]{2,1,0:T(8,128)S(1)} %bitcast.3, bf16[512,64]{1,0:T(8,128)(2,1)S(1)} %copy.12.density_ref, s32[2,4]{1,0:T(2,128)S(1)} %copy-done.8), custom_call_target="tpu_custom_call" | custom-call | tf_op jit(solution)/shard_map/first/pallas_call | solution.py:226
  19.0 8.0 %all-gather.1 = bf16[1024,128]{1,0:T(8,128)(2,1)S(1)} all-gather(bf16[512,128]{1,0:T(8,128)(2,1)S(1)} %get-tuple-element.9), channel_id=3, replica_groups={{0,8},{2,10},{4,12},{6,14},{9,17},{11,19},{13,21},{15,23},{16,24},{18,2..., dimensions={0}, use_global_device_ids=true | all-gather | bytes 393216 | tf_op jit(solution)/shard_map/all_gather | solution.py:243
  27.0 2.0 %all-gather.2 = bf16[1024,128]{1,0:T(8,128)(2,1)S(1)} all-gather(bf16[512,128]{1,0:T(8,128)(2,1)S(1)} %fusion), channel_id=4, replica_groups={{0,1},{2,3},{4,5},{6,7},{8,9},{10,11},{12,13},{14,15},{16,17},{18,19},{..., dimensions={0}, use_global_device_ids=true | all-gather | bytes 393216 | tf_op jit(solution)/shard_map/all_gather | solution.py:246
  29.1 8.2 %all-gather.3 = bf16[1280,128]{1,0:T(8,128)(2,1)S(1)} all-gather(bf16[640,128]{1,0:T(8,128)(2,1)S(1)} %pad_maximum_fusion), channel_id=5, replica_groups={{2,4},{0,6},{3,5},{1,7},{10,12},{8,14},{11,13},{9,15},{18,20},{16,22},{..., dimensions={0}, use_global_device_ids=true | all-gather | bytes 491520 | tf_op jit(solution)/shard_map/all_gather | solution.py:248
  37.3 2.9 %second.1 = (bf16[512,64]{1,0:T(8,128)(2,1)S(1)}, bf16[256,128]{1,0:T(8,128)(2,1)S(1)}, f32[256,128]{1,0:T(8,128)S(1)}) custom-call(bf16[2,640,128]{2,1,0:T(8,128)(2,1)S(1)} %bitcast.2), custom_call_target="tpu_custom_call" | custom-call | tf_op jit(solution)/shard_map/second/pallas_call | solution.py:249
  40.2 0.7 %copy.13 = bf16[512,64]{0,1:T(8,128)(2,1)} copy(bf16[512,64]{1,0:T(8,128)(2,1)S(1)} %get-tuple-element.14) | data formatting | bytes 131072
  41.0 7.4 %all-gather.4 = bf16[512,128]{1,0:T(8,128)(2,1)S(1)} all-gather(bf16[256,128]{1,0:T(8,128)(2,1)S(1)} %get-tuple-element.13), channel_id=6, replica_groups={{0,8},{2,10},{4,12},{6,14},{9,17},{11,19},{13,21},{15,23},{16,24},{18,2..., dimensions={0}, use_global_device_ids=true | all-gather | bytes 196608 | tf_op jit(solution)/shard_map/all_gather | solution.py:264
  48.4 2.0 %all-gather.5 = f32[512,128]{1,0:T(8,128)S(1)} all-gather(f32[256,128]{1,0:T(8,128)S(1)} %convert_add_fusion.1), channel_id=7, replica_groups={{0,1},{2,3},{4,5},{6,7},{8,9},{10,11},{12,13},{14,15},{16,17},{18,19},{..., dimensions={0}, use_global_device_ids=true | all-gather | bytes 393216 | tf_op jit(solution)/shard_map/all_gather | solution.py:266
  50.4 0.1 fusion.2
  50.6 0.7 %copy.14 = bf16[512,64]{0,1:T(8,128)(2,1)} copy(bf16[512,64]{1,0:T(8,128)(2,1)S(1)} %pad_maximum_fusion.1) | data formatting | bytes 131072
  (15 shorter events, 0.2 us)
Async XLA Ops:
  0.6 0.7 %copy-start.7 = (f32[1,1,1024]{2,1,0:T(1,128)S(1)}, f32[1,1,1024]{2,1,0:T(1,128)}, u32[]{:S(2)}) copy-start(f32[1,1,1024]{2,1,0:T(1,128)} %refs_7_.1) | copy-start | bytes 12292
  0.7 0.7 %copy-start.6 = (s32[1,1,1024]{2,1,0:T(1,128)S(1)}, s32[1,1,1024]{2,1,0:T(1,128)}, u32[]{:S(2)}) copy-start(s32[1,1,1024]{2,1,0:T(1,128)} %refs_6_.1) | copy-start | bytes 12292
  0.7 0.7 %copy-start.5 = (s32[1,1,1024]{2,1,0:T(1,128)S(1)}, s32[1,1,1024]{2,1,0:T(1,128)}, u32[]{:S(2)}) copy-start(s32[1,1,1024]{2,1,0:T(1,128)} %refs_5_.1) | copy-start | bytes 12292
  0.7 0.7 %copy-start.4 = (s32[1,1,1024]{2,1,0:T(1,128)S(1)}, s32[1,1,1024]{2,1,0:T(1,128)}, u32[]{:S(2)}) copy-start(s32[1,1,1024]{2,1,0:T(1,128)} %refs_4_.1) | copy-start | bytes 12292
  0.7 0.7 %copy-start.3 = (f32[1,1,1024]{2,1,0:T(1,128)S(1)}, f32[1,1,1024]{2,1,0:T(1,128)}, u32[]{:S(2)}) copy-start(f32[1,1,1024]{2,1,0:T(1,128)} %refs_3_.1) | copy-start | bytes 12292
  0.7 0.7 %copy-start.2 = (s32[1,1,1024]{2,1,0:T(1,128)S(1)}, s32[1,1,1024]{2,1,0:T(1,128)}, u32[]{:S(2)}) copy-start(s32[1,1,1024]{2,1,0:T(1,128)} %refs_2_.1) | copy-start | bytes 12292
  0.7 0.7 %copy-start.1 = (s32[1,1,1024]{2,1,0:T(1,128)S(1)}, s32[1,1,1024]{2,1,0:T(1,128)}, u32[]{:S(2)}) copy-start(s32[1,1,1024]{2,1,0:T(1,128)} %refs_1_.1) | copy-start | bytes 12292
  0.7 0.7 %copy-start = (s32[1,1,1024]{2,1,0:T(1,128)S(1)}, s32[1,1,1024]{2,1,0:T(1,128)}, u32[]{:S(2)}) copy-start(s32[1,1,1024]{2,1,0:T(1,128)} %refs_0_.1) | copy-start | bytes 12292
  1.4 13.8 %copy-start.9 = (bf16[512,64]{0,1:T(8,128)(2,1)S(1)}, bf16[512,64]{0,1:T(8,128)(2,1)}, u32[]{:S(2)}) copy-start(bf16[512,64]{0,1:T(8,128)(2,1)} %param.10) | copy-start | bytes 196612
  15.2 0.7 %copy-start.8 = (s32[2,4]{1,0:T(2,128)S(1)}, s32[2,4]{1,0:T(2,128)}, u32[]{:S(2)}) copy-start(s32[2,4]{1,0:T(2,128)} %offsets_ref.1) | copy-start | bytes 100

commit v2 on v1

v2 whole, which is shorter than its diff:
```python
import functools

import jax
import jax.numpy as jnp
from jax import lax
from jax.experimental import pallas as pl
from jax.experimental.pallas import tpu as pltpu
from jax.sharding import PartitionSpec as P

F32 = jnp.float32
BF16 = jnp.bfloat16
BLOCK = 256
COLS = 64
WIDTH = 4
AXES = ("box", "seg")


def place():
    box = lax.axis_index("box")
    core = lax.axis_index("seg") % 2
    pair = box // 2
    return pair, box % 2, core, 1 - (pair + core) % 2


def pair_groups(boxes):
    pairs = boxes // 2
    groups = []
    for first in range(pairs):
        second = (first + 1) % pairs
        for chip in range(4):
            core = first % 2
            groups.append([first * 8 + chip * 2 + core, second * 8 + chip * 2 + core])
    return groups


def core_groups(boxes):
    return [[2 * chip, 2 * chip + 1] for chip in range(boxes * 2)]


def half_groups(boxes):
    groups = []
    for pair in range(boxes // 2):
        for core in range(2):
            groups.append([pair * 8 + 2 + core, pair * 8 + 4 + core])
            groups.append([pair * 8 + core, pair * 8 + 6 + core])
    return groups


def iota(shape, dim):
    return lax.broadcasted_iota(jnp.int32, shape, dim)


def across(left, right):
    return lax.dot_general(left, right, (((1,), (1,)), ((), ())), preferred_element_type=F32)


def sort_kernel(*refs):
    *ins, offsets_ref, out_ref, marks_ref, pick_ref = refs
    rows = out_ref.shape[1]
    count = ins[0].shape[-1]
    step = 64
    lane = iota((step, count), 1).astype(F32)
    offs = offsets_ref[...].astype(F32)
    marks_ref[...] = jnp.concatenate(
        [jnp.broadcast_to(offs[j : j + 1, s : s + 1], (1, 128)) for j in range(2) for s in range(WIDTH)], axis=0
    )
    for day in range(2):
        start, slot, end, weight = (ref[0] for ref in ins[4 * day : 4 * day + 4])
        for at in range(0, rows, step):
            hit = start == iota((step, count), 0) + at
            first = jnp.min(jnp.where(hit, lane, float(count)), axis=1, keepdims=True)
            last = jnp.max(jnp.where(hit, lane, -1.0), axis=1, keepdims=True)
            pick_ref[at : at + step, :] = jnp.where(lane == first, 1.0, 0.0).astype(BF16)
            pick_ref[rows + at : rows + at + step, :] = jnp.where(lane == last, 1.0, 0.0).astype(BF16)
        high = weight.astype(BF16).astype(F32)
        middle = (weight - high).astype(BF16).astype(F32)
        low = weight - high - middle
        zero = jnp.zeros_like(weight)
        load = jnp.concatenate(
            [end.astype(F32), slot.astype(F32), high, middle, low, zero, zero, zero], axis=0
        ).astype(BF16)
        got = across(load, pick_ref[...])
        target = got[1:2] * float(BLOCK) + got[0:1]
        total = got[2:3] + got[3:4] + got[4:5]
        out_ref[4 * day : 4 * day + 4, :] = jnp.concatenate(
            [target[:, :rows], target[:, rows:], total[:, :rows], total[:, rows:]], axis=0
        )


def split_work(blocks, half_only, ahead):
    places = []
    for block in blocks:
        place_of = jnp.where(block < 0, 0, jnp.where(block >= 4, 1, 2))
        if half_only is not None:
            place_of = jnp.where(((block >> 1) & 1) == half_only, place_of, 3)
        places.append(place_of)
    behind, front, inside = (sum((p == kind).astype(jnp.int32) for p in places) for kind in range(3))
    share = jnp.clip(((behind + front + inside + 1) >> 1) - front, 0, inside)
    mine, seen = [], 0
    for p in places:
        is_inside = p == 2
        taker = jnp.where(seen < share, 1, 0)
        mine.append(jnp.logical_or(p == ahead, jnp.logical_and(is_inside, taker == ahead)))
        seen = seen + is_inside.astype(jnp.int32)
    return places, mine


def push_block(key_ref, weight_ref, part, s, density, counts_ref, sum_ref):
    cut = slice(BLOCK * part, BLOCK * part + BLOCK)
    step = 16
    keys, weights = [], []
    for k in range(key_ref.shape[0]):
        key = key_ref[k : k + 1, cut] - float(s * BLOCK)
        keys.append(jnp.broadcast_to(key, (step, BLOCK)).astype(BF16))
        weights.append(jnp.broadcast_to(weight_ref[k : k + 1, cut], (step, BLOCK)).astype(BF16))
    first = iota((step, BLOCK), 0).astype(F32)
    zero = jnp.zeros((step, BLOCK), BF16)
    for at in range(0, BLOCK, step):
        ends = (first + float(at)).astype(BF16)
        total = None
        for key, weight in zip(keys, weights):
            term = jnp.where(key == ends, weight, zero)
            total = term if total is None else total + term
        counts_ref[at : at + step, :] = total
    sum_ref[...] += across(density, counts_ref[...])


def first_kernel(lists_ref, density_ref, marks_ref, side_ref, own_ref, meta_ref, key_ref, weight_ref, counts_ref, sums_ref):
    pair, half, core, ahead = place()
    lanes = lists_ref.shape[0]
    rows = lists_ref.shape[2]
    marks = marks_ref[...]
    whole = marks.astype(jnp.int32)
    blocks = [2 * half + i // WIDTH + whole[i, 0] for i in range(2 * WIDTH)]
    places, mine = split_work(blocks, None, ahead)
    for day in range(2):
        keys = jnp.concatenate([lists_ref[lane, 4 * day : 4 * day + 2, :] for lane in range(lanes)], axis=0)
        weights = jnp.concatenate([lists_ref[lane, 4 * day + 2 : 4 * day + 4, :] for lane in range(lanes)], axis=0)
        weights = weights / jnp.sum(weights, axis=0, keepdims=True)
        if day == 0:
            key_ref[...] = keys
            weight_ref[...] = weights
        else:
            slots = jnp.floor(keys * (1.0 / BLOCK))
            ends = keys - slots * float(BLOCK)
            wide = jnp.concatenate([marks, marks], axis=1)
            for part in range(2):
                cut = slice(BLOCK * part, BLOCK * part + BLOCK)
                meta_ref[32 * part : 32 * part + 32, :] = jnp.concatenate(
                    [ends[:, cut], slots[:, cut], weights[:, cut], wide], axis=0
                ).astype(BF16)
    sums_ref[...] = jnp.zeros_like(sums_ref)
    for j in range(2):
        for s in range(WIDTH):
            number = WIDTH * j + s

            @pl.when(mine[number])
            def _():
                at = jnp.where(places[number] == 2, 1, 0)
                density = density_ref[:, BLOCK * j : BLOCK * j + BLOCK]
                push_block(key_ref, weight_ref, j, s, density, counts_ref, sums_ref.at[at, blocks[number] & 3])

    for spot in range(4):
        cut = slice(COLS * spot, COLS * spot + COLS)
        side_ref[cut, :] = sums_ref[0, spot].astype(BF16)
        own_ref[cut, :] = sums_ref[1, spot]


def second_kernel(parts_ref, density_ref, side_ref, own_ref, stage_ref, key_ref, weight_ref, from_ref, counts_ref, sums_ref, sem):
    pair, half, core, ahead = place()
    wide = 4 * COLS
    total = parts_ref[0, :wide, :].astype(F32) + parts_ref[1, :wide, :].astype(F32)
    for j in range(4):
        from_ref[j] = total[COLS * j : COLS * j + COLS].astype(BF16)
    for part in range(2):
        stage_ref[:, BLOCK * part : BLOCK * part + BLOCK] = from_ref[2 * half + part]
    store = pltpu.make_async_copy(stage_ref, density_ref, sem)
    store.start()
    blocks = []
    for group in range(2):
        for part in range(2):
            piece = parts_ref[group, wide + 32 * part : wide + 32 * part + 32, :].astype(F32)
            cut = slice(BLOCK * part, BLOCK * part + BLOCK)
            key_ref[group, :, cut] = piece[8:16] * float(BLOCK) + piece[0:8]
            weight_ref[group, :, cut] = piece[16:24]
            if part == 0:
                whole = piece[24:32, :128].astype(jnp.int32)
                blocks += [2 * group + i // WIDTH + whole[i, 0] for i in range(2 * WIDTH)]
    places, mine = split_work(blocks, half, ahead)
    sums_ref[...] = jnp.zeros_like(sums_ref)
    for j in range(4):
        for s in range(WIDTH):
            number = WIDTH * j + s

            @pl.when(mine[number])
            def _():
                at = jnp.where(places[number] == 2, 1, 0)
                push_block(
                    key_ref.at[j >> 1], weight_ref.at[j >> 1], j & 1, s, from_ref[j], counts_ref, sums_ref.at[at, blocks[number] & 1]
                )

    for spot in range(2):
        cut = slice(COLS * spot, COLS * spot + COLS)
        side_ref[cut, :] = sums_ref[0, spot].astype(BF16)
        own_ref[cut, :] = sums_ref[1, spot]
    store.wait()


def last_kernel(both_ref, density_ref, stage_ref, sem):
    total = (both_ref[0] + both_ref[1]).astype(BF16)
    stage_ref[:, :BLOCK] = total[:COLS]
    stage_ref[:, BLOCK:] = total[COLS:]
    store = pltpu.make_async_copy(stage_ref, density_ref, sem)
    store.start()
    store.wait()


VMEM = pl.BlockSpec(memory_space=pltpu.VMEM)
ANY = pl.BlockSpec(memory_space=pl.ANY)


def call(kernel, name, outs, out_specs, scratch):
    return pl.pallas_call(
        kernel,
        out_shape=outs,
        out_specs=out_specs,
        scratch_shapes=scratch,
        compiler_params=pltpu.CompilerParams(vmem_limit_bytes=32 * 1024 * 1024),
        name=name,
    )


def shaped(*shape, dtype=F32):
    return jax.ShapeDtypeStruct(shape, dtype)


def body(density, offsets, *segments):
    boxes = lax.axis_size("box")
    rows = density.shape[0]
    count = segments[0].shape[-1]
    gather = functools.partial(lax.all_gather, axis_name=AXES)
    pair, half, core, ahead = place()

    lists, marks = call(
        sort_kernel,
        "sort",
        (shaped(8, rows), shaped(8, 128)),
        (VMEM, VMEM),
        [pltpu.VMEM((2 * rows, count), BF16)],
    )(*[member.reshape(1, 1, count) for member in segments], offsets)
    lists = lax.all_gather(lists, "seg")
    side, own, meta = call(
        first_kernel,
        "first",
        (shaped(4 * COLS, BLOCK, dtype=BF16), shaped(4 * COLS, BLOCK), shaped(64, BLOCK, dtype=BF16)),
        (VMEM, VMEM, VMEM),
        [
            pltpu.VMEM((8, rows), F32),
            pltpu.VMEM((8, rows), F32),
            pltpu.VMEM((BLOCK, BLOCK), BF16),
            pltpu.VMEM((2, 4, COLS, BLOCK), F32),
        ],
    )(lists, density.T, marks)
    sides = gather(side, axis_index_groups=pair_groups(boxes))
    came = jnp.where(ahead == 1, sides[1], sides[0])
    mixed = (own + came.astype(F32)).astype(BF16)
    both = gather(mixed, axis_index_groups=core_groups(boxes))
    summed = (both[0].astype(F32) + both[1].astype(F32)).astype(BF16)
    parts = gather(jnp.concatenate([summed, meta], axis=0), axis_index_groups=half_groups(boxes))
    density_one, side, own = call(
        second_kernel,
        "second",
        (shaped(COLS, rows, dtype=BF16), shaped(2 * COLS, BLOCK, dtype=BF16), shaped(2 * COLS, BLOCK)),
        (ANY, VMEM, VMEM),
        [
            pltpu.VMEM((COLS, rows), BF16),
            pltpu.VMEM((2, 8, rows), F32),
            pltpu.VMEM((2, 8, rows), F32),
            pltpu.VMEM((4, COLS, BLOCK), BF16),
            pltpu.VMEM((BLOCK, BLOCK), BF16),
            pltpu.VMEM((2, 2, COLS, BLOCK), F32),
            pltpu.SemaphoreType.DMA,
        ],
    )(parts)
    sides = gather(side, axis_index_groups=pair_groups(boxes))
    came = jnp.where(ahead == 1, sides[1], sides[0])
    both = gather(own + came.astype(F32), axis_index_groups=core_groups(boxes))
    density_two = call(
        last_kernel,
        "last",
        shaped(COLS, rows, dtype=BF16),
        ANY,
        [pltpu.VMEM((COLS, rows), BF16), pltpu.SemaphoreType.DMA],
    )(both)
    return density_one.T, density_two.T


def solution(mesh):
    boxed = P("box", None)
    lined = P("box", "seg", None)
    return jax.shard_map(
        body,
        mesh=mesh,
        in_specs=(boxed, boxed) + (lined,) * 8,
        out_specs=(boxed, boxed),
        check_vma=False,
    )
```

time: 51.5 us -> 46.2 us (0.90)
  Pallas kernels: 7.79 us -> 4.52 us
  local copies, waits for them, and re-layouts: 2.93 us -> 0.71 us
    pallas_call x3 -> x4, Pallas kernels: 7.79 us -> 4.52 us  [the longest x1 1.8 us: body(): call(sort_kernel, 'sort', (shaped(8, rows), shaped(8, 128)), (VMEM, VMEM)...]
    unnamed x23 -> x20, local copies, waits for them, and re-layouts: 2.84 us -> 0.71 us
    all_gather x2, blocking collectives: 15.4 us -> 16.4 us  [body(): sides = gather(side, axis_index_groups=pair_groups(boxes))]
    all_gather x1, blocking collectives: 8.22 us -> 7.55 us  [body(): gather(jnp.concatenate([summed, meta], axis=0), axis_index_groups=half_gr...]
where the time goes in v2:
time: 46.2 us; the launch traced here: 46 us
  blocking collectives  39.9 us (86%)
  Pallas kernels  4.52 us (10%)
  between operations  0.8 us (2%)
  local copies, waits for them, and re-layouts  0.71 us (2%)
    all_gather x2, blocking collectives, body(): sides = gather(side, axis_index_groups=pair_groups(boxes))  16.4 us
    all_gather x1, blocking collectives, body(): lists = lax.all_gather(lists, 'seg')  12 us
    all_gather x1, blocking collectives, body(): gather(jnp.concatenate([summed, meta], axis=0), axis_index_groups=half_gr...  7.55 us
    all_gather x1, blocking collectives, body(): both = gather(own + came.astype(F32), axis_index_groups=core_groups(boxes))  1.99 us
    all_gather x1, blocking collectives, body(): both = gather(mixed, axis_index_groups=core_groups(boxes))  1.99 us
    pallas_call x1, Pallas kernels, body(): call(sort_kernel, 'sort', (shaped(8, rows), shaped(8, 128)), (VMEM, VMEM)...  1.8 us
    pallas_call x1, Pallas kernels, body(): call(first_kernel, 'first', (shaped(4 * COLS, BLOCK, dtype=BF16), shaped(...  1.13 us
    pallas_call x1, Pallas kernels, body(): call(second_kernel, 'second', (shaped(COLS, rows, dtype=BF16), shaped(2 *...  0.95 us

profile of v2, /device:TPU:1, one launch (start us, length us, event | category | flops | bytes accessed | tf_op | source)
XLA Modules:
  0.0 46.0 jit_solution(17437899311784618592)
XLA Ops:
  0.6 0.0 copy-start.9
  0.7 0.0 copy-start.8
  0.7 0.0 copy-start.7
  0.7 0.0 copy-start.6
  0.7 0.0 copy-start.5
  0.8 0.6 %copy-done.9 = s32[2,4]{1,0:T(2,128)S(1)} copy-done((s32[2,4]{1,0:T(2,128)S(1)}, s32[2,4]{1,0:T(2,128)}, u32[]{:S(2)}) %copy-start.9) | copy-done | bytes 56
  1.3 0.0 copy-done.8
  1.4 0.0 copy-done.7
  1.4 0.0 copy-done.6
  1.4 0.0 copy-done.5
  1.4 0.0 copy-done.4
  1.4 0.0 copy-done.3
  1.4 0.0 copy-done.1
  1.4 0.0 copy-done.2
  1.5 1.8 %sort.1 = (f32[8,512]{1,0:T(8,128)S(1)}, f32[8,128]{1,0:T(8,128)S(1)}) custom-call(s32[1,1,1024]{2,1,0:T(1,128)S(1)} %copy-done.1, s32[1,1,1024]{2,1,0:T(1,128)S(1)} %copy-done.2, s32[1,1,1024]{2,1,0:T(1,128)S(1)} %copy-done.3, f32[1,1,1024]{2,1,0:T(1,128)S(1)} %copy-done.4, s32[1,1,1024]{2,1,0:T(1,128)S(1)} %copy-done.5, s32[1,1,1024]{2,1,0:T(1,128)S(1)} %copy-done.6, ...), custom_call_target="tpu_custom_call" | custom-call | tf_op jit(solution)/shard_map/sort/pallas_call | solution.py:244
  3.3 12.0 %all-gather = f32[32,512]{1,0:T(8,128)S(1)} all-gather(f32[8,512]{1,0:T(8,128)S(1)} %get-tuple-element.10), channel_id=2, replica_groups=mesh['box'=128,'seg'=4] {'seg'}, dimensions={0}, use_global_device_ids=true | all-gather | bytes 81920 | tf_op jit(solution)/shard_map/all_gather | solution.py:251
  15.2 1.1 %first.1 = (bf16[256,256]{1,0:T(8,128)(2,1)S(1)}, f32[256,256]{1,0:T(8,128)S(1)}, bf16[64,256]{1,0:T(8,128)(2,1)S(1)}) custom-call(f32[4,8,512]{2,1,0:T(8,128)S(1)} %bitcast.8, bf16[64,512]{1,0:T(8,128)(2,1)S(1)} %bitcast.9, f32[8,128]{1,0:T(8,128)S(1)} %get-tuple-element.11.marks_ref), custom_call_target="tpu_custom_call" | custom-call | tf_op jit(solution)/shard_map/first/pallas_call | solution.py:252
  16.4 9.3 %all-gather.1 = bf16[512,256]{1,0:T(8,128)(2,1)S(1)} all-gather(bf16[256,256]{1,0:T(8,128)(2,1)S(1)} %get-tuple-element.13), channel_id=3, replica_groups={{0,8},{2,10},{4,12},{6,14},{9,17},{11,19},{13,21},{15,23},{16,24},{18,2..., dimensions={0}, use_global_device_ids=true | all-gather | bytes 393216 | tf_op jit(solution)/shard_map/all_gather | solution.py:264
  25.7 2.0 %all-gather.2 = bf16[512,256]{1,0:T(8,128)(2,1)S(1)} all-gather(bf16[256,256]{1,0:T(8,128)(2,1)S(1)} %fusion), channel_id=4, replica_groups={{0,1},{2,3},{4,5},{6,7},{8,9},{10,11},{12,13},{14,15},{16,17},{18,19},{..., dimensions={0}, use_global_device_ids=true | all-gather | bytes 393216 | tf_op jit(solution)/shard_map/all_gather | solution.py:267
  27.8 7.5 %all-gather.3 = bf16[640,256]{1,0:T(8,128)(2,1)S(1)} all-gather(bf16[320,256]{1,0:T(8,128)(2,1)S(1)} %pad_maximum_fusion), channel_id=5, replica_groups={{2,4},{0,6},{3,5},{1,7},{10,12},{8,14},{11,13},{9,15},{18,20},{16,22},{..., dimensions={0}, use_global_device_ids=true | all-gather | bytes 491520 | tf_op jit(solution)/shard_map/all_gather | solution.py:269
  35.3 0.9 %second.1 = (bf16[64,512]{1,0:T(8,128)(2,1)}, bf16[128,256]{1,0:T(8,128)(2,1)S(1)}, f32[128,256]{1,0:T(8,128)S(1)}) custom-call(bf16[2,320,256]{2,1,0:T(8,128)(2,1)S(1)} %bitcast.6), custom_call_target="tpu_custom_call" | custom-call | tf_op jit(solution)/shard_map/second/pallas_call | solution.py:270
  36.3 7.1 %all-gather.4 = bf16[256,256]{1,0:T(8,128)(2,1)S(1)} all-gather(bf16[128,256]{1,0:T(8,128)(2,1)S(1)} %get-tuple-element.17), channel_id=6, replica_groups={{0,8},{2,10},{4,12},{6,14},{9,17},{11,19},{13,21},{15,23},{16,24},{18,2..., dimensions={0}, use_global_device_ids=true | all-gather | bytes 196608 | tf_op jit(solution)/shard_map/all_gather | solution.py:285
  43.4 2.0 %all-gather.5 = f32[256,256]{1,0:T(8,128)S(1)} all-gather(f32[128,256]{1,0:T(8,128)S(1)} %convert_add_fusion.1), channel_id=7, replica_groups={{0,1},{2,3},{4,5},{6,7},{8,9},{10,11},{12,13},{14,15},{16,17},{18,19},{..., dimensions={0}, use_global_device_ids=true | all-gather | bytes 393216 | tf_op jit(solution)/shard_map/all_gather | solution.py:287
  45.4 0.7 %last.1 = bf16[64,512]{1,0:T(8,128)(2,1)} custom-call(f32[2,128,256]{2,1,0:T(8,128)S(1)} %bitcast.7), custom_call_target="tpu_custom_call" | custom-call | tf_op jit(solution)/shard_map/last/pallas_call | solution.py:288
  (10 shorter events, 0.1 us)
Async XLA Ops:
  0.6 0.7 %copy-start.9 = (s32[2,4]{1,0:T(2,128)S(1)}, s32[2,4]{1,0:T(2,128)}, u32[]{:S(2)}) copy-start(s32[2,4]{1,0:T(2,128)} %refs_8_.1) | copy-start | bytes 100
  0.7 0.7 %copy-start.8 = (f32[1,1,1024]{2,1,0:T(1,128)S(1)}, f32[1,1,1024]{2,1,0:T(1,128)}, u32[]{:S(2)}) copy-start(f32[1,1,1024]{2,1,0:T(1,128)} %refs_7_.1) | copy-start | bytes 12292
  0.7 0.7 %copy-start.7 = (s32[1,1,1024]{2,1,0:T(1,128)S(1)}, s32[1,1,1024]{2,1,0:T(1,128)}, u32[]{:S(2)}) copy-start(s32[1,1,1024]{2,1,0:T(1,128)} %refs_6_.1) | copy-start | bytes 12292
  0.7 0.7 %copy-start.6 = (s32[1,1,1024]{2,1,0:T(1,128)S(1)}, s32[1,1,1024]{2,1,0:T(1,128)}, u32[]{:S(2)}) copy-start(s32[1,1,1024]{2,1,0:T(1,128)} %refs_5_.1) | copy-start | bytes 12292
  0.7 0.7 %copy-start.5 = (s32[1,1,1024]{2,1,0:T(1,128)S(1)}, s32[1,1,1024]{2,1,0:T(1,128)}, u32[]{:S(2)}) copy-start(s32[1,1,1024]{2,1,0:T(1,128)} %refs_4_.1) | copy-start | bytes 12292
  0.7 0.7 %copy-start.4 = (f32[1,1,1024]{2,1,0:T(1,128)S(1)}, f32[1,1,1024]{2,1,0:T(1,128)}, u32[]{:S(2)}) copy-start(f32[1,1,1024]{2,1,0:T(1,128)} %refs_3_.1) | copy-start | bytes 12292
  0.7 0.7 %copy-start.3 = (s32[1,1,1024]{2,1,0:T(1,128)S(1)}, s32[1,1,1024]{2,1,0:T(1,128)}, u32[]{:S(2)}) copy-start(s32[1,1,1024]{2,1,0:T(1,128)} %refs_2_.1) | copy-start | bytes 12292
  0.7 0.7 %copy-start.1 = (s32[1,1,1024]{2,1,0:T(1,128)S(1)}, s32[1,1,1024]{2,1,0:T(1,128)}, u32[]{:S(2)}) copy-start(s32[1,1,1024]{2,1,0:T(1,128)} %refs_0_.1) | copy-start | bytes 12292
  0.7 0.7 %copy-start.2 = (s32[1,1,1024]{2,1,0:T(1,128)S(1)}, s32[1,1,1024]{2,1,0:T(1,128)}, u32[]{:S(2)}) copy-start(s32[1,1,1024]{2,1,0:T(1,128)} %refs_1_.1) | copy-start | bytes 12292
  0.8 14.5 %copy-start = (bf16[512,64]{0,1:T(8,128)(2,1)S(1)}, bf16[512,64]{0,1:T(8,128)(2,1)}, u32[]{:S(2)}) copy-start(bf16[512,64]{0,1:T(8,128)(2,1)} %param.10) | copy-start | bytes 196612

commit v3 on v2

--- a/solution.py
+++ b/solution.py
@@ -40,9 +40,8 @@
 def half_groups(boxes):
     groups = []
     for pair in range(boxes // 2):
-        for core in range(2):
-            groups.append([pair * 8 + 2 + core, pair * 8 + 4 + core])
-            groups.append([pair * 8 + core, pair * 8 + 6 + core])
+        groups.append([pair * 8 + i for i in (2, 3, 4, 5)])
+        groups.append([pair * 8 + i for i in (0, 1, 6, 7)])
     return groups
 
 
@@ -144,11 +143,8 @@
             slots = jnp.floor(keys * (1.0 / BLOCK))
             ends = keys - slots * float(BLOCK)
             wide = jnp.concatenate([marks, marks], axis=1)
-            for part in range(2):
-                cut = slice(BLOCK * part, BLOCK * part + BLOCK)
-                meta_ref[32 * part : 32 * part + 32, :] = jnp.concatenate(
-                    [ends[:, cut], slots[:, cut], weights[:, cut], wide], axis=0
-                ).astype(BF16)
+            picked = [jnp.where(core == 0, one[:, :BLOCK], one[:, BLOCK:]) for one in (ends, slots, weights)]
+            meta_ref[...] = jnp.concatenate(picked + [wide], axis=0).astype(BF16)
     sums_ref[...] = jnp.zeros_like(sums_ref)
     for j in range(2):
         for s in range(WIDTH):
@@ -169,23 +165,22 @@
 def second_kernel(parts_ref, density_ref, side_ref, own_ref, stage_ref, key_ref, weight_ref, from_ref, counts_ref, sums_ref, sem):
     pair, half, core, ahead = place()
     wide = 4 * COLS
-    total = parts_ref[0, :wide, :].astype(F32) + parts_ref[1, :wide, :].astype(F32)
     for j in range(4):
-        from_ref[j] = total[COLS * j : COLS * j + COLS].astype(BF16)
+        cut = slice(COLS * j, COLS * j + COLS)
+        one, two, three, four = (parts_ref[i, cut, :].astype(F32) for i in range(4))
+        from_ref[j] = ((one + two) + (three + four)).astype(BF16)
     for part in range(2):
         stage_ref[:, BLOCK * part : BLOCK * part + BLOCK] = from_ref[2 * half + part]
     store = pltpu.make_async_copy(stage_ref, density_ref, sem)
     store.start()
     blocks = []
-    for group in range(2):
-        for part in range(2):
-            piece = parts_ref[group, wide + 32 * part : wide + 32 * part + 32, :].astype(F32)
-            cut = slice(BLOCK * part, BLOCK * part + BLOCK)
-            key_ref[group, :, cut] = piece[8:16] * float(BLOCK) + piece[0:8]
-            weight_ref[group, :, cut] = piece[16:24]
-            if part == 0:
-                whole = piece[24:32, :128].astype(jnp.int32)
-                blocks += [2 * group + i // WIDTH + whole[i, 0] for i in range(2 * WIDTH)]
+    for j in range(4):
+        piece = parts_ref[j, wide : wide + 32, :].astype(F32)
+        cut = slice(BLOCK * (j & 1), BLOCK * (j & 1) + BLOCK)
+        key_ref[j >> 1, :, cut] = piece[8:16] * float(BLOCK) + piece[0:8]
+        weight_ref[j >> 1, :, cut] = piece[16:24]
+        whole = piece[24:32, :128].astype(jnp.int32)
+        blocks += [j + whole[WIDTH * (j & 1) + s, 0] for s in range(WIDTH)]
     places, mine = split_work(blocks, half, ahead)
     sums_ref[...] = jnp.zeros_like(sums_ref)
     for j in range(4):
@@ -252,7 +247,7 @@
     side, own, meta = call(
         first_kernel,
         "first",
-        (shaped(4 * COLS, BLOCK, dtype=BF16), shaped(4 * COLS, BLOCK), shaped(64, BLOCK, dtype=BF16)),
+        (shaped(4 * COLS, BLOCK, dtype=BF16), shaped(4 * COLS, BLOCK), shaped(32, BLOCK, dtype=BF16)),
         (VMEM, VMEM, VMEM),
         [
             pltpu.VMEM((8, rows), F32),
@@ -264,9 +259,7 @@
     sides = gather(side, axis_index_groups=pair_groups(boxes))
     came = jnp.where(ahead == 1, sides[1], sides[0])
     mixed = (own + came.astype(F32)).astype(BF16)
-    both = gather(mixed, axis_index_groups=core_groups(boxes))
-    summed = (both[0].astype(F32) + both[1].astype(F32)).astype(BF16)
-    parts = gather(jnp.concatenate([summed, meta], axis=0), axis_index_groups=half_groups(boxes))
+    parts = gather(jnp.concatenate([mixed, meta], axis=0), axis_index_groups=half_groups(boxes))
     density_one, side, own = call(
         second_kernel,
         "second",

time: 46.2 us -> 45.7 us (0.989)
  blocking collectives: 39.9 us -> 39.2 us
    all_gather x2 -> x1, blocking collectives: 9.54 us -> 8.86 us  [body(): gather(jnp.concatenate([mixed, meta], axis=0), axis_index_groups=half_gro...]
where the time goes in v3:
time: 45.7 us; the launch traced here: 45.5 us
  blocking collectives  39.2 us (86%)
  Pallas kernels  4.77 us (10%)
  between operations  0.8 us (2%)
  local copies, waits for them, and re-layouts  0.71 us (2%)
    all_gather x2, blocking collectives, body(): sides = gather(side, axis_index_groups=pair_groups(boxes))  16.4 us
    all_gather x1, blocking collectives, body(): lists = lax.all_gather(lists, 'seg')  12 us
    all_gather x1, blocking collectives, body(): gather(jnp.concatenate([mixed, meta], axis=0), axis_index_groups=half_gro...  8.86 us
    all_gather x1, blocking collectives, body(): both = gather(own + came.astype(F32), axis_index_groups=core_groups(boxes))  1.99 us
    pallas_call x1, Pallas kernels, body(): call(sort_kernel, 'sort', (shaped(8, rows), shaped(8, 128)), (VMEM, VMEM)...  1.8 us
    pallas_call x1, Pallas kernels, body(): call(first_kernel, 'first', (shaped(4 * COLS, BLOCK, dtype=BF16), shaped(...  1.35 us
    pallas_call x1, Pallas kernels, body(): call(second_kernel, 'second', (shaped(COLS, rows, dtype=BF16), shaped(2 *...  0.97 us

profile of v3, /device:TPU:1, one launch (start us, length us, event | category | flops | bytes accessed | tf_op | source)
XLA Modules:
  0.0 45.5 jit_solution(15894463383889226003)
XLA Ops:
  0.6 0.0 copy-start.9
  0.7 0.0 copy-start.8
  0.7 0.0 copy-start.7
  0.7 0.0 copy-start.6
  0.7 0.0 copy-start.5
  0.7 0.0 copy-start.4
  0.8 0.6 %copy-done.9 = s32[2,4]{1,0:T(2,128)S(1)} copy-done((s32[2,4]{1,0:T(2,128)S(1)}, s32[2,4]{1,0:T(2,128)}, u32[]{:S(2)}) %copy-start.9) | copy-done | bytes 56
  1.3 0.0 copy-done.8
  1.4 0.0 copy-done.7
  1.4 0.0 copy-done.6
  1.4 0.0 copy-done.5
  1.4 0.0 copy-done.4
  1.4 0.0 copy-done.3
  1.4 0.0 copy-done.1
  1.4 0.0 copy-done.2
  1.5 1.8 %sort.1 = (f32[8,512]{1,0:T(8,128)S(1)}, f32[8,128]{1,0:T(8,128)S(1)}) custom-call(s32[1,1,1024]{2,1,0:T(1,128)S(1)} %copy-done.1, s32[1,1,1024]{2,1,0:T(1,128)S(1)} %copy-done.2, s32[1,1,1024]{2,1,0:T(1,128)S(1)} %copy-done.3, f32[1,1,1024]{2,1,0:T(1,128)S(1)} %copy-done.4, s32[1,1,1024]{2,1,0:T(1,128)S(1)} %copy-done.5, s32[1,1,1024]{2,1,0:T(1,128)S(1)} %copy-done.6, ...), custom_call_target="tpu_custom_call" | custom-call | tf_op jit(solution)/shard_map/sort/pallas_call | solution.py:239
  3.3 12.0 %all-gather = f32[32,512]{1,0:T(8,128)S(1)} all-gather(f32[8,512]{1,0:T(8,128)S(1)} %get-tuple-element.10), channel_id=2, replica_groups=mesh['box'=128,'seg'=4] {'seg'}, dimensions={0}, use_global_device_ids=true | all-gather | bytes 81920 | tf_op jit(solution)/shard_map/all_gather | solution.py:246
  15.2 1.4 %first.1 = (bf16[256,256]{1,0:T(8,128)(2,1)S(1)}, f32[256,256]{1,0:T(8,128)S(1)}, bf16[32,256]{1,0:T(8,128)(2,1)S(1)}) custom-call(f32[4,8,512]{2,1,0:T(8,128)S(1)} %bitcast.8, bf16[64,512]{1,0:T(8,128)(2,1)S(1)} %bitcast.9, f32[8,128]{1,0:T(8,128)S(1)} %get-tuple-element.11.marks_ref), custom_call_target="tpu_custom_call" | custom-call | tf_op jit(solution)/shard_map/first/pallas_call | solution.py:247
  16.6 9.1 %all-gather.1 = bf16[512,256]{1,0:T(8,128)(2,1)S(1)} all-gather(bf16[256,256]{1,0:T(8,128)(2,1)S(1)} %get-tuple-element.13), channel_id=3, replica_groups={{0,8},{2,10},{4,12},{6,14},{9,17},{11,19},{13,21},{15,23},{16,24},{18,2..., dimensions={0}, use_global_device_ids=true | all-gather | bytes 393216 | tf_op jit(solution)/shard_map/all_gather | solution.py:259
  25.7 8.9 %all-gather.2 = bf16[1152,256]{1,0:T(8,128)(2,1)S(1)} all-gather(bf16[288,256]{1,0:T(8,128)(2,1)S(1)} %pad_maximum_fusion), channel_id=4, replica_groups={{2,3,4,5},{0,1,6,7},{10,11,12,13},{8,9,14,15},{18,19,20,21},{16,17,22,2..., dimensions={0}, use_global_device_ids=true | all-gather | bytes 737280 | tf_op jit(solution)/shard_map/all_gather | solution.py:262
  34.6 1.0 %second.1 = (bf16[64,512]{1,0:T(8,128)(2,1)}, bf16[128,256]{1,0:T(8,128)(2,1)S(1)}, f32[128,256]{1,0:T(8,128)S(1)}) custom-call(bf16[4,288,256]{2,1,0:T(8,128)(2,1)S(1)} %bitcast.6), custom_call_target="tpu_custom_call" | custom-call | tf_op jit(solution)/shard_map/second/pallas_call | solution.py:263
  35.6 7.3 %all-gather.3 = bf16[256,256]{1,0:T(8,128)(2,1)S(1)} all-gather(bf16[128,256]{1,0:T(8,128)(2,1)S(1)} %get-tuple-element.17), channel_id=5, replica_groups={{0,8},{2,10},{4,12},{6,14},{9,17},{11,19},{13,21},{15,23},{16,24},{18,2..., dimensions={0}, use_global_device_ids=true | all-gather | bytes 196608 | tf_op jit(solution)/shard_map/all_gather | solution.py:278
  42.9 2.0 %all-gather.4 = f32[256,256]{1,0:T(8,128)S(1)} all-gather(f32[128,256]{1,0:T(8,128)S(1)} %convert_add_fusion.1), channel_id=6, replica_groups={{0,1},{2,3},{4,5},{6,7},{8,9},{10,11},{12,13},{14,15},{16,17},{18,19},{..., dimensions={0}, use_global_device_ids=true | all-gather | bytes 393216 | tf_op jit(solution)/shard_map/all_gather | solution.py:280
  44.9 0.7 %last.1 = bf16[64,512]{1,0:T(8,128)(2,1)} custom-call(f32[2,128,256]{2,1,0:T(8,128)S(1)} %bitcast.7), custom_call_target="tpu_custom_call" | custom-call | tf_op jit(solution)/shard_map/last/pallas_call | solution.py:281
  (8 shorter events, 0.1 us)
Async XLA Ops:
  0.6 0.7 %copy-start.9 = (s32[2,4]{1,0:T(2,128)S(1)}, s32[2,4]{1,0:T(2,128)}, u32[]{:S(2)}) copy-start(s32[2,4]{1,0:T(2,128)} %refs_8_.1) | copy-start | bytes 100
  0.7 0.7 %copy-start.8 = (f32[1,1,1024]{2,1,0:T(1,128)S(1)}, f32[1,1,1024]{2,1,0:T(1,128)}, u32[]{:S(2)}) copy-start(f32[1,1,1024]{2,1,0:T(1,128)} %refs_7_.1) | copy-start | bytes 12292
  0.7 0.7 %copy-start.7 = (s32[1,1,1024]{2,1,0:T(1,128)S(1)}, s32[1,1,1024]{2,1,0:T(1,128)}, u32[]{:S(2)}) copy-start(s32[1,1,1024]{2,1,0:T(1,128)} %refs_6_.1) | copy-start | bytes 12292
  0.7 0.7 %copy-start.6 = (s32[1,1,1024]{2,1,0:T(1,128)S(1)}, s32[1,1,1024]{2,1,0:T(1,128)}, u32[]{:S(2)}) copy-start(s32[1,1,1024]{2,1,0:T(1,128)} %refs_5_.1) | copy-start | bytes 12292
  0.7 0.7 %copy-start.5 = (s32[1,1,1024]{2,1,0:T(1,128)S(1)}, s32[1,1,1024]{2,1,0:T(1,128)}, u32[]{:S(2)}) copy-start(s32[1,1,1024]{2,1,0:T(1,128)} %refs_4_.1) | copy-start | bytes 12292
  0.7 0.7 %copy-start.4 = (f32[1,1,1024]{2,1,0:T(1,128)S(1)}, f32[1,1,1024]{2,1,0:T(1,128)}, u32[]{:S(2)}) copy-start(f32[1,1,1024]{2,1,0:T(1,128)} %refs_3_.1) | copy-start | bytes 12292
  0.7 0.7 %copy-start.3 = (s32[1,1,1024]{2,1,0:T(1,128)S(1)}, s32[1,1,1024]{2,1,0:T(1,128)}, u32[]{:S(2)}) copy-start(s32[1,1,1024]{2,1,0:T(1,128)} %refs_2_.1) | copy-start | bytes 12292
  0.7 0.7 %copy-start.1 = (s32[1,1,1024]{2,1,0:T(1,128)S(1)}, s32[1,1,1024]{2,1,0:T(1,128)}, u32[]{:S(2)}) copy-start(s32[1,1,1024]{2,1,0:T(1,128)} %refs_0_.1) | copy-start | bytes 12292
  0.7 0.7 %copy-start.2 = (s32[1,1,1024]{2,1,0:T(1,128)S(1)}, s32[1,1,1024]{2,1,0:T(1,128)}, u32[]{:S(2)}) copy-start(s32[1,1,1024]{2,1,0:T(1,128)} %refs_1_.1) | copy-start | bytes 12292
  0.8 14.5 %copy-start = (bf16[512,64]{0,1:T(8,128)(2,1)S(1)}, bf16[512,64]{0,1:T(8,128)(2,1)}, u32[]{:S(2)}) copy-start(bf16[512,64]{0,1:T(8,128)(2,1)} %param.10) | copy-start | bytes 196612

commit v4 on v3

v4 whole, which is shorter than its diff:
```python
import functools

import jax
import jax.numpy as jnp
from jax import lax
from jax.experimental import pallas as pl
from jax.experimental.pallas import tpu as pltpu
from jax.sharding import PartitionSpec as P

F32 = jnp.float32
BF16 = jnp.bfloat16
BLOCK = 256
COLS = 64
WIDTH = 4
GROUP = 4
AXES = ("box", "seg")


def place():
    box = lax.axis_index("box")
    core = lax.axis_index("seg") % 2
    pair = box // 2
    return pair, box % 2, core, 1 - (pair + core) % 2


def pair_groups(boxes):
    pairs = boxes // 2
    groups = []
    for first in range(pairs):
        second = (first + 1) % pairs
        for chip in range(4):
            core = first % 2
            groups.append([first * 8 + chip * 2 + core, second * 8 + chip * 2 + core])
    return groups


def core_groups(boxes):
    return [[2 * chip, 2 * chip + 1] for chip in range(boxes * 2)]


def half_groups(boxes):
    groups = []
    for pair in range(boxes // 2):
        groups.append([pair * 8 + i for i in (2, 3, 4, 5)])
        groups.append([pair * 8 + i for i in (0, 1, 6, 7)])
    return groups


def iota(shape, dim):
    return lax.broadcasted_iota(jnp.int32, shape, dim)


def across(left, right):
    return lax.dot_general(left, right, (((1,), (1,)), ((), ())), preferred_element_type=F32)


def sort_kernel(*refs):
    *ins, offsets_ref, out_ref, marks_ref = refs
    offs = offsets_ref[...].astype(F32)
    marks_ref[...] = jnp.concatenate(
        [jnp.broadcast_to(offs[j : j + 1, s : s + 1], (1, 128)) for j in range(2) for s in range(WIDTH)], axis=0
    )
    chunks = ins[0].shape[0]
    past = float(128 * chunks)
    below = iota((8, 128), 0).astype(F32)
    wants = [(iota((8, 128), 1) + 128 * q).astype(F32) for q in range(4)]
    for day in range(2):
        start, slot, end, weight = (ref[...] for ref in ins[4 * day : 4 * day + 4])
        turned = start.astype(F32).T
        firsts = [jnp.full((8, 128), past, F32)] * 4
        lasts = [jnp.full((8, 128), -1.0, F32)] * 4
        for c in range(chunks):
            wide = jnp.broadcast_to(turned[:, c : c + 1], (128, 128))
            for i in range(16):
                at = below + float(128 * c + 8 * i)
                for q in range(4):
                    hit = wide[8 * i : 8 * i + 8] == wants[q]
                    firsts[q] = jnp.minimum(firsts[q], jnp.where(hit, at, past))
                    lasts[q] = jnp.where(hit, at, lasts[q])
        firsts = [jnp.min(one, axis=0, keepdims=True) for one in firsts]
        lasts = [jnp.max(one, axis=0, keepdims=True) for one in lasts]
        spots = jnp.concatenate(firsts + lasts, axis=0)
        chunk = jnp.floor(spots * (1.0 / 128))
        lane = (spots - chunk * 128.0).astype(jnp.int32)
        for field, values in enumerate((slot.astype(F32) * float(BLOCK) + end.astype(F32), weight)):
            got = None
            for c in range(chunks):
                row = jnp.broadcast_to(values[c : c + 1], (8, 128))
                part = jnp.take_along_axis(row, lane, axis=1, mode="promise_in_bounds")
                got = part if got is None else jnp.where(chunk == float(c), part, got)
            at = 16 * day + 8 * field
            out_ref[at : at + 8, :] = got


def split_work(blocks, half_only, ahead):
    places = []
    for block in blocks:
        place_of = jnp.where(block < 0, 0, jnp.where(block >= 4, 1, 2))
        if half_only is not None:
            place_of = jnp.where(((block >> 1) & 1) == half_only, place_of, 3)
        places.append(place_of)
    behind, front, inside = (sum((p == kind).astype(jnp.int32) for p in places) for kind in range(3))
    share = jnp.clip(((behind + front + inside + 1) >> 1) - front, 0, inside)
    mine, seen = [], 0
    for p in places:
        is_inside = p == 2
        taker = jnp.where(seen < share, 1, 0)
        mine.append(jnp.logical_or(p == ahead, jnp.logical_and(is_inside, taker == ahead)))
        seen = seen + is_inside.astype(jnp.int32)
    return places, mine


def fold(tiles, part):
    low = (iota((8, 128), 0) & 3) < 2
    one, two = tiles
    return jnp.where(
        low,
        jnp.where(part == 0, one, pltpu.roll(one, 6, 0)),
        jnp.where(part == 0, pltpu.roll(two, 2, 0), two),
    )


def list_work(work_ref, blocks, places, mine, spots):
    done = jnp.int32(0)
    for number, (block, place_of, take) in enumerate(zip(blocks, places, mine)):
        at = jnp.where(place_of == 2, spots, 0) + (block & (spots - 1))
        work_ref[done] = number * 16 + at
        done = done + take.astype(jnp.int32)
    for i in range(GROUP):
        work_ref[done + i] = 2 * spots
    return done


def push_blocks(work_ref, done, key_ref, weight_ref, from_ref, counts_ref, sums_ref):
    step = 16
    first = iota((step, BLOCK), 0).astype(F32)
    zero = jnp.zeros((step, BLOCK), BF16)

    @pl.loop(0, (done + GROUP - 1) // GROUP)
    def _(group):
        items = [work_ref[group * GROUP + i] for i in range(GROUP)]
        for i, item in enumerate(items):
            j = item >> 6
            base = (((item >> 4) & 3) * BLOCK).astype(F32)
            keys, weights = [], []
            for side in range(2):
                key_tile = key_ref[2 * j + side] - base
                weight_tile = weight_ref[2 * j + side]
                for row in (0, 2, 4, 6):
                    two = [slice(row + t, row + t + 1) for t in range(2)]
                    wide = [
                        jnp.concatenate([jnp.broadcast_to(tile[one, :], (step, 128)) for one in two], axis=1).astype(BF16)
                        for tile in (key_tile, weight_tile)
                    ]
                    keys.append(wide[0])
                    weights.append(wide[1])
            for at in range(0, BLOCK, step):
                ends = (first + float(at)).astype(BF16)
                total = None
                for key, weight in zip(keys, weights):
                    term = jnp.where(key == ends, weight, zero)
                    total = term if total is None else total + term
                counts_ref[i, at : at + step, :] = total
        pushed = [across(from_ref[item >> 6], counts_ref[i]) for i, item in enumerate(items)]
        for item, one in zip(items, pushed):
            sums_ref[item & 15] += one


def first_kernel(lists_ref, density_ref, marks_ref, side_ref, own_ref, meta_ref, key_ref, weight_ref, from_ref, counts_ref, sums_ref, work_ref):
    pair, half, core, ahead = place()
    lanes = lists_ref.shape[0]
    marks = marks_ref[...]
    whole = marks.astype(jnp.int32)
    blocks = [2 * half + i // WIDTH + whole[i, 0] for i in range(2 * WIDTH)]
    places, mine = split_work(blocks, None, ahead)
    done = list_work(work_ref, blocks, places, mine, 4)
    for j in range(2):
        from_ref[j] = density_ref[:, BLOCK * j : BLOCK * j + BLOCK]
    for day in range(2):
        keys = [lists_ref[lane, 16 * day : 16 * day + 8, :] for lane in range(lanes)]
        weights = [lists_ref[lane, 16 * day + 8 : 16 * day + 16, :] for lane in range(lanes)]
        total = weights[0] + weights[1] + weights[2] + weights[3]
        total = total + pltpu.roll(total, 4, 0)
        weights = [weight / total for weight in weights]
        if day == 0:
            for j in range(2):
                for side in range(2):
                    key_ref[2 * j + side] = fold(keys[2 * side : 2 * side + 2], j)
                    weight_ref[2 * j + side] = fold(weights[2 * side : 2 * side + 2], j)
        else:
            slots = [jnp.floor(key * (1.0 / BLOCK)) for key in keys]
            ends = [key - slot * float(BLOCK) for key, slot in zip(keys, slots)]
            pieces = [
                jnp.concatenate([fold(field[:2], core), fold(field[2:], core)], axis=1) for field in (ends, slots, weights)
            ]
            meta_ref[...] = jnp.concatenate(pieces + [jnp.concatenate([marks, marks], axis=1)], axis=0).astype(BF16)
    sums_ref[...] = jnp.zeros_like(sums_ref)
    push_blocks(work_ref, done, key_ref, weight_ref, from_ref, counts_ref, sums_ref)
    for spot in range(4):
        cut = slice(COLS * spot, COLS * spot + COLS)
        side_ref[cut, :] = sums_ref[spot].astype(BF16)
        own_ref[cut, :] = sums_ref[4 + spot]


def second_kernel(parts_ref, density_ref, side_ref, own_ref, stage_ref, key_ref, weight_ref, from_ref, counts_ref, sums_ref, work_ref, sem):
    pair, half, core, ahead = place()
    wide = 4 * COLS
    blocks = []
    for j in range(4):
        piece = parts_ref[j, wide : wide + 32, :].astype(F32)
        keys = piece[8:16] * float(BLOCK) + piece[0:8]
        for side in range(2):
            cut = slice(128 * side, 128 * side + 128)
            key_ref[2 * j + side] = keys[:, cut]
            weight_ref[2 * j + side] = piece[16:24, cut]
        whole = piece[24:32, :128].astype(jnp.int32)
        blocks += [j + whole[WIDTH * (j & 1) + s, 0] for s in range(WIDTH)]
    places, mine = split_work(blocks, half, ahead)
    done = list_work(work_ref, blocks, places, mine, 2)
    for j in range(4):
        cut = slice(COLS * j, COLS * j + COLS)
        one, two, three, four = (parts_ref[i, cut, :].astype(F32) for i in range(4))
        from_ref[j] = ((one + two) + (three + four)).astype(BF16)
    for part in range(2):
        stage_ref[:, BLOCK * part : BLOCK * part + BLOCK] = from_ref[2 * half + part]
    store = pltpu.make_async_copy(stage_ref, density_ref, sem)
    store.start()
    sums_ref[...] = jnp.zeros_like(sums_ref)
    push_blocks(work_ref, done, key_ref, weight_ref, from_ref, counts_ref, sums_ref)
    for spot in range(2):
        cut = slice(COLS * spot, COLS * spot + COLS)
        side_ref[cut, :] = sums_ref[spot].astype(BF16)
        own_ref[cut, :] = sums_ref[2 + spot]
    store.wait()


def last_kernel(both_ref, density_ref, stage_ref, sem):
    total = (both_ref[0] + both_ref[1]).astype(BF16)
    stage_ref[:, :BLOCK] = total[:COLS]
    stage_ref[:, BLOCK:] = total[COLS:]
    store = pltpu.make_async_copy(stage_ref, density_ref, sem)
    store.start()
    store.wait()


VMEM = pl.BlockSpec(memory_space=pltpu.VMEM)
ANY = pl.BlockSpec(memory_space=pl.ANY)


def call(kernel, name, outs, out_specs, scratch):
    return pl.pallas_call(
        kernel,
        out_shape=outs,
        out_specs=out_specs,
        scratch_shapes=scratch,
        compiler_params=pltpu.CompilerParams(vmem_limit_bytes=32 * 1024 * 1024),
        name=name,
    )


def shaped(*shape, dtype=F32):
    return jax.ShapeDtypeStruct(shape, dtype)


def body(density, offsets, *segments):
    boxes = lax.axis_size("box")
    rows = density.shape[0]
    count = segments[0].shape[-1]
    gather = functools.partial(lax.all_gather, axis_name=AXES)
    pair, half, core, ahead = place()

    lists, marks = call(
        sort_kernel,
        "sort",
        (shaped(32, 128), shaped(8, 128)),
        (VMEM, VMEM),
        [],
    )(*[member.reshape(count // 128, 128) for member in segments], offsets)
    lists = lax.all_gather(lists, "seg")
    side, own, meta = call(
        first_kernel,
        "first",
        (shaped(4 * COLS, BLOCK, dtype=BF16), shaped(4 * COLS, BLOCK), shaped(32, BLOCK, dtype=BF16)),
        (VMEM, VMEM, VMEM),
        [
            pltpu.VMEM((4, 8, 128), F32),
            pltpu.VMEM((4, 8, 128), F32),
            pltpu.VMEM((2, COLS, BLOCK), BF16),
            pltpu.VMEM((GROUP, BLOCK, BLOCK), BF16),
            pltpu.VMEM((9, COLS, BLOCK), F32),
            pltpu.SMEM((2 * WIDTH + GROUP,), jnp.int32),
        ],
    )(lists, density.T, marks)
    sides = gather(side, axis_index_groups=pair_groups(boxes))
    came = jnp.where(ahead == 1, sides[1], sides[0])
    mixed = (own + came.astype(F32)).astype(BF16)
    parts = gather(jnp.concatenate([mixed, meta], axis=0), axis_index_groups=half_groups(boxes))
    density_one, side, own = call(
        second_kernel,
        "second",
        (shaped(COLS, rows, dtype=BF16), shaped(2 * COLS, BLOCK, dtype=BF16), shaped(2 * COLS, BLOCK)),
        (ANY, VMEM, VMEM),
        [
            pltpu.VMEM((COLS, rows), BF16),
            pltpu.VMEM((8, 8, 128), F32),
            pltpu.VMEM((8, 8, 128), F32),
            pltpu.VMEM((4, COLS, BLOCK), BF16),
            pltpu.VMEM((GROUP, BLOCK, BLOCK), BF16),
            pltpu.VMEM((5, COLS, BLOCK), F32),
            pltpu.SMEM((4 * WIDTH + GROUP,), jnp.int32),
            pltpu.SemaphoreType.DMA,
        ],
    )(parts)
    sides = gather(side, axis_index_groups=pair_groups(boxes))
    came = jnp.where(ahead == 1, sides[1], sides[0])
    both = gather(own + came.astype(F32), axis_index_groups=core_groups(boxes))
    density_two = call(
        last_kernel,
        "last",
        shaped(COLS, rows, dtype=BF16),
        ANY,
        [pltpu.VMEM((COLS, rows), BF16), pltpu.SemaphoreType.DMA],
    )(both)
    return density_one.T, density_two.T


def solution(mesh):
    boxed = P("box", None)
    lined = P("box", "seg", None)
    return jax.shard_map(
        body,
        mesh=mesh,
        in_specs=(boxed, boxed) + (lined,) * 8,
        out_specs=(boxed, boxed),
        check_vma=False,
    )
```

time: 45.7 us -> 45.3 us (level)
  Pallas kernels: 4.77 us -> 4.05 us
    pallas_call x1, Pallas kernels: 1.8 us -> 1.18 us  [body(): call(sort_kernel, 'sort', (shaped(32, 128), shaped(8, 128)), (VMEM, VMEM)...]
    pallas_call x1, Pallas kernels: 1.35 us -> 0.75 us  [body(): call(first_kernel, 'first', (shaped(4 * COLS, BLOCK, dtype=BF16), shaped(...]
    pallas_call x1, Pallas kernels: 0.97 us -> 1.48 us  [body(): call(second_kernel, 'second', (shaped(COLS, rows, dtype=BF16), shaped(2 *...]
where the time goes in v4:
time: 45.3 us
  blocking collectives  39.6 us (87%)
  Pallas kernels  4.05 us (9%)
  between operations  0.8 us (2%)
  local copies, waits for them, and re-layouts  0.72 us (2%)
    all_gather x2, blocking collectives, body(): sides = gather(side, axis_index_groups=pair_groups(boxes))  16.4 us
    all_gather x1, blocking collectives, body(): lists = lax.all_gather(lists, 'seg')  12 us
    all_gather x1, blocking collectives, body(): gather(jnp.concatenate([mixed, meta], axis=0), axis_index_groups=half_gro...  9.26 us
    all_gather x1, blocking collectives, body(): both = gather(own + came.astype(F32), axis_index_groups=core_groups(boxes))  1.99 us
    pallas_call x1, Pallas kernels, body(): call(second_kernel, 'second', (shaped(COLS, rows, dtype=BF16), shaped(2 *...  1.48 us
    pallas_call x1, Pallas kernels, body(): call(sort_kernel, 'sort', (shaped(32, 128), shaped(8, 128)), (VMEM, VMEM)...  1.18 us

profile of v4, /device:TPU:1, one launch (start us, length us, event | category | flops | bytes accessed | tf_op | source)
XLA Modules:
  0.0 45.3 jit_solution(12184080484133684958)
XLA Ops:
  0.7 0.0 copy-start.9
  0.7 0.0 copy-start.4
  0.7 0.0 copy-start.3
  0.7 0.0 copy-start.1
  0.8 0.0 copy-start.2
  0.8 0.0 copy-start
  0.8 0.6 %copy-done.9 = s32[2,4]{1,0:T(2,128)S(1)} copy-done((s32[2,4]{1,0:T(2,128)S(1)}, s32[2,4]{1,0:T(2,128)}, u32[]{:S(2)}) %copy-start.9) | copy-done | bytes 56
  1.3 0.0 copy-done.8
  1.4 0.0 copy-done.7
  1.4 0.0 copy-done.6
  1.4 0.0 copy-done.5
  1.4 0.0 copy-done.4
  1.4 0.0 copy-done.3
  1.4 0.0 copy-done.1
  1.5 0.0 copy-done.2
  1.5 1.2 %sort.1 = (f32[32,128]{1,0:T(8,128)S(1)}, f32[8,128]{1,0:T(8,128)S(1)}) custom-call(s32[8,128]{1,0:T(8,128)S(1)} %bitcast.18, s32[8,128]{1,0:T(8,128)S(1)} %bitcast.19, s32[8,128]{1,0:T(8,128)S(1)} %bitcast.20, f32[8,128]{1,0:T(8,128)S(1)} %bitcast.21, s32[8,128]{1,0:T(8,128)S(1)} %bitcast.22, s32[8,128]{1,0:T(8,128)S(1)} %bitcast.23, ...), custom_call_target="tpu_custom_call" | custom-call | tf_op jit(solution)/shard_map/sort/pallas_call | solution.py:272
  2.7 12.0 %all-gather = f32[128,128]{1,0:T(8,128)S(1)} all-gather(f32[32,128]{1,0:T(8,128)S(1)} %get-tuple-element.10), channel_id=2, replica_groups=mesh['box'=128,'seg'=4] {'seg'}, dimensions={0}, use_global_device_ids=true | all-gather | bytes 81920 | tf_op jit(solution)/shard_map/all_gather | solution.py:279
  14.6 0.7 %first.1 = (bf16[256,256]{1,0:T(8,128)(2,1)S(1)}, f32[256,256]{1,0:T(8,128)S(1)}, bf16[32,256]{1,0:T(8,128)(2,1)S(1)}) custom-call(f32[4,32,128]{2,1,0:T(8,128)S(1)} %bitcast.16, bf16[64,512]{1,0:T(8,128)(2,1)S(1)} %bitcast.17, f32[8,128]{1,0:T(8,128)S(1)} %get-tuple-element.11.marks_ref), custom_call_target="tpu_custom_call" | custom-call | tf_op jit(solution)/shard_map/first/pallas_call | solution.py:280
  15.4 9.3 %all-gather.1 = bf16[512,256]{1,0:T(8,128)(2,1)S(1)} all-gather(bf16[256,256]{1,0:T(8,128)(2,1)S(1)} %get-tuple-element.13), channel_id=3, replica_groups={{0,8},{2,10},{4,12},{6,14},{9,17},{11,19},{13,21},{15,23},{16,24},{18,2..., dimensions={0}, use_global_device_ids=true | all-gather | bytes 393216 | tf_op jit(solution)/shard_map/all_gather | solution.py:294
  24.7 9.3 %all-gather.2 = bf16[1152,256]{1,0:T(8,128)(2,1)S(1)} all-gather(bf16[288,256]{1,0:T(8,128)(2,1)S(1)} %pad_maximum_fusion), channel_id=4, replica_groups={{2,3,4,5},{0,1,6,7},{10,11,12,13},{8,9,14,15},{18,19,20,21},{16,17,22,2..., dimensions={0}, use_global_device_ids=true | all-gather | bytes 737280 | tf_op jit(solution)/shard_map/all_gather | solution.py:297
  34.0 1.5 %second.1 = (bf16[64,512]{1,0:T(8,128)(2,1)}, bf16[128,256]{1,0:T(8,128)(2,1)S(1)}, f32[128,256]{1,0:T(8,128)S(1)}) custom-call(bf16[4,288,256]{2,1,0:T(8,128)(2,1)S(1)} %bitcast.14), custom_call_target="tpu_custom_call" | custom-call | tf_op jit(solution)/shard_map/second/pallas_call | solution.py:298
  35.5 7.1 %all-gather.3 = bf16[256,256]{1,0:T(8,128)(2,1)S(1)} all-gather(bf16[128,256]{1,0:T(8,128)(2,1)S(1)} %get-tuple-element.17), channel_id=5, replica_groups={{0,8},{2,10},{4,12},{6,14},{9,17},{11,19},{13,21},{15,23},{16,24},{18,2..., dimensions={0}, use_global_device_ids=true | all-gather | bytes 196608 | tf_op jit(solution)/shard_map/all_gather | solution.py:314
  42.6 2.0 %all-gather.4 = f32[256,256]{1,0:T(8,128)S(1)} all-gather(f32[128,256]{1,0:T(8,128)S(1)} %convert_add_fusion.1), channel_id=6, replica_groups={{0,1},{2,3},{4,5},{6,7},{8,9},{10,11},{12,13},{14,15},{16,17},{18,19},{..., dimensions={0}, use_global_device_ids=true | all-gather | bytes 393216 | tf_op jit(solution)/shard_map/all_gather | solution.py:316
  44.6 0.7 %last.1 = bf16[64,512]{1,0:T(8,128)(2,1)} custom-call(f32[2,128,256]{2,1,0:T(8,128)S(1)} %bitcast.15), custom_call_target="tpu_custom_call" | custom-call | tf_op jit(solution)/shard_map/last/pallas_call | solution.py:317
  (8 shorter events, 0.1 us)
Async XLA Ops:
  0.7 0.7 %copy-start.9 = (s32[2,4]{1,0:T(2,128)S(1)}, s32[2,4]{1,0:T(2,128)}, u32[]{:S(2)}) copy-start(s32[2,4]{1,0:T(2,128)} %refs_8_.1) | copy-start | bytes 100
  0.7 0.7 %copy-start.8 = (f32[1,1,1024]{2,1,0:T(1,128)S(1)}, f32[1,1,1024]{2,1,0:T(1,128)}, u32[]{:S(2)}) copy-start(f32[1,1,1024]{2,1,0:T(1,128)} %param.19) | copy-start | bytes 12292
  0.7 0.7 %copy-start.7 = (s32[1,1,1024]{2,1,0:T(1,128)S(1)}, s32[1,1,1024]{2,1,0:T(1,128)}, u32[]{:S(2)}) copy-start(s32[1,1,1024]{2,1,0:T(1,128)} %param.18) | copy-start | bytes 12292
  0.7 0.7 %copy-start.6 = (s32[1,1,1024]{2,1,0:T(1,128)S(1)}, s32[1,1,1024]{2,1,0:T(1,128)}, u32[]{:S(2)}) copy-start(s32[1,1,1024]{2,1,0:T(1,128)} %param.17) | copy-start | bytes 12292
  0.7 0.7 %copy-start.5 = (s32[1,1,1024]{2,1,0:T(1,128)S(1)}, s32[1,1,1024]{2,1,0:T(1,128)}, u32[]{:S(2)}) copy-start(s32[1,1,1024]{2,1,0:T(1,128)} %param.16) | copy-start | bytes 12292
  0.7 0.7 %copy-start.4 = (f32[1,1,1024]{2,1,0:T(1,128)S(1)}, f32[1,1,1024]{2,1,0:T(1,128)}, u32[]{:S(2)}) copy-start(f32[1,1,1024]{2,1,0:T(1,128)} %param.15) | copy-start | bytes 12292
  0.7 0.7 %copy-start.3 = (s32[1,1,1024]{2,1,0:T(1,128)S(1)}, s32[1,1,1024]{2,1,0:T(1,128)}, u32[]{:S(2)}) copy-start(s32[1,1,1024]{2,1,0:T(1,128)} %param.14) | copy-start | bytes 12292
  0.7 0.7 %copy-start.1 = (s32[1,1,1024]{2,1,0:T(1,128)S(1)}, s32[1,1,1024]{2,1,0:T(1,128)}, u32[]{:S(2)}) copy-start(s32[1,1,1024]{2,1,0:T(1,128)} %param.12) | copy-start | bytes 12292
  0.8 0.7 %copy-start.2 = (s32[1,1,1024]{2,1,0:T(1,128)S(1)}, s32[1,1,1024]{2,1,0:T(1,128)}, u32[]{:S(2)}) copy-start(s32[1,1,1024]{2,1,0:T(1,128)} %param.13) | copy-start | bytes 12292
  0.8 13.9 %copy-start = (bf16[512,64]{0,1:T(8,128)(2,1)S(1)}, bf16[512,64]{0,1:T(8,128)(2,1)}, u32[]{:S(2)}) copy-start(bf16[512,64]{0,1:T(8,128)(2,1)} %param.10) | copy-start | bytes 196612

commit v5 on v4

--- a/solution.py
+++ b/solution.py
@@ -12,7 +12,7 @@
 BLOCK = 256
 COLS = 64
 WIDTH = 4
-GROUP = 4
+GROUPS = (4, 5)
 AXES = ("box", "seg")
 
 
@@ -64,6 +64,7 @@
     past = float(128 * chunks)
     below = iota((8, 128), 0).astype(F32)
     wants = [(iota((8, 128), 1) + 128 * q).astype(F32) for q in range(4)]
+    found = []
     for day in range(2):
         start, slot, end, weight = (ref[...] for ref in ins[4 * day : 4 * day + 4])
         turned = start.astype(F32).T
@@ -82,14 +83,14 @@
         spots = jnp.concatenate(firsts + lasts, axis=0)
         chunk = jnp.floor(spots * (1.0 / 128))
         lane = (spots - chunk * 128.0).astype(jnp.int32)
-        for field, values in enumerate((slot.astype(F32) * float(BLOCK) + end.astype(F32), weight)):
+        for values in (end.astype(F32), slot.astype(F32), weight):
             got = None
             for c in range(chunks):
                 row = jnp.broadcast_to(values[c : c + 1], (8, 128))
                 part = jnp.take_along_axis(row, lane, axis=1, mode="promise_in_bounds")
                 got = part if got is None else jnp.where(chunk == float(c), part, got)
-            at = 16 * day + 8 * field
-            out_ref[at : at + 8, :] = got
+            found.append(got)
+    out_ref[...] = jnp.concatenate(found, axis=0).astype(BF16)
 
 
 def split_work(blocks, half_only, ahead):
@@ -120,13 +121,13 @@
     )
 
 
-def list_work(work_ref, blocks, places, mine, spots):
+def list_work(work_ref, blocks, places, mine, spots, size):
     done = jnp.int32(0)
     for number, (block, place_of, take) in enumerate(zip(blocks, places, mine)):
         at = jnp.where(place_of == 2, spots, 0) + (block & (spots - 1))
         work_ref[done] = number * 16 + at
         done = done + take.astype(jnp.int32)
-    for i in range(GROUP):
+    for i in range(size):
         work_ref[done + i] = 2 * spots
     return done
 
@@ -136,9 +137,11 @@
     first = iota((step, BLOCK), 0).astype(F32)
     zero = jnp.zeros((step, BLOCK), BF16)
 
-    @pl.loop(0, (done + GROUP - 1) // GROUP)
+    size = counts_ref.shape[0]
+
+    @pl.loop(0, (done + size - 1) // size)
     def _(group):
-        items = [work_ref[group * GROUP + i] for i in range(GROUP)]
+        items = [work_ref[group * size + i] for i in range(size)]
         for i, item in enumerate(items):
             j = item >> 6
             base = (((item >> 4) & 3) * BLOCK).astype(F32)
@@ -173,23 +176,24 @@
     whole = marks.astype(jnp.int32)
     blocks = [2 * half + i // WIDTH + whole[i, 0] for i in range(2 * WIDTH)]
     places, mine = split_work(blocks, None, ahead)
-    done = list_work(work_ref, blocks, places, mine, 4)
+    done = list_work(work_ref, blocks, places, mine, 4, counts_ref.shape[0])
     for j in range(2):
         from_ref[j] = density_ref[:, BLOCK * j : BLOCK * j + BLOCK]
+    lists = [lists_ref[lane].astype(F32) for lane in range(lanes)]
     for day in range(2):
-        keys = [lists_ref[lane, 16 * day : 16 * day + 8, :] for lane in range(lanes)]
-        weights = [lists_ref[lane, 16 * day + 8 : 16 * day + 16, :] for lane in range(lanes)]
+        ends, slots, weights = (
+            [one[24 * day + 8 * field : 24 * day + 8 * field + 8] for one in lists] for field in range(3)
+        )
         total = weights[0] + weights[1] + weights[2] + weights[3]
         total = total + pltpu.roll(total, 4, 0)
         weights = [weight / total for weight in weights]
         if day == 0:
+            keys = [slot * float(BLOCK) + end for slot, end in zip(slots, ends)]
             for j in range(2):
                 for side in range(2):
                     key_ref[2 * j + side] = fold(keys[2 * side : 2 * side + 2], j)
                     weight_ref[2 * j + side] = fold(weights[2 * side : 2 * side + 2], j)
         else:
-            slots = [jnp.floor(key * (1.0 / BLOCK)) for key in keys]
-            ends = [key - slot * float(BLOCK) for key, slot in zip(keys, slots)]
             pieces = [
                 jnp.concatenate([fold(field[:2], core), fold(field[2:], core)], axis=1) for field in (ends, slots, weights)
             ]
@@ -216,7 +220,7 @@
         whole = piece[24:32, :128].astype(jnp.int32)
         blocks += [j + whole[WIDTH * (j & 1) + s, 0] for s in range(WIDTH)]
     places, mine = split_work(blocks, half, ahead)
-    done = list_work(work_ref, blocks, places, mine, 2)
+    done = list_work(work_ref, blocks, places, mine, 2, counts_ref.shape[0])
     for j in range(4):
         cut = slice(COLS * j, COLS * j + COLS)
         one, two, three, four = (parts_ref[i, cut, :].astype(F32) for i in range(4))
@@ -235,7 +239,7 @@
 
 
 def last_kernel(both_ref, density_ref, stage_ref, sem):
-    total = (both_ref[0] + both_ref[1]).astype(BF16)
+    total = (both_ref[0].astype(F32) + both_ref[1].astype(F32)).astype(BF16)
     stage_ref[:, :BLOCK] = total[:COLS]
     stage_ref[:, BLOCK:] = total[COLS:]
     store = pltpu.make_async_copy(stage_ref, density_ref, sem)
@@ -272,7 +276,7 @@
     lists, marks = call(
         sort_kernel,
         "sort",
-        (shaped(32, 128), shaped(8, 128)),
+        (shaped(48, 128, dtype=BF16), shaped(8, 128)),
         (VMEM, VMEM),
         [],
     )(*[member.reshape(count // 128, 128) for member in segments], offsets)
@@ -286,9 +290,9 @@
             pltpu.VMEM((4, 8, 128), F32),
             pltpu.VMEM((4, 8, 128), F32),
             pltpu.VMEM((2, COLS, BLOCK), BF16),
-            pltpu.VMEM((GROUP, BLOCK, BLOCK), BF16),
+            pltpu.VMEM((GROUPS[0], BLOCK, BLOCK), BF16),
             pltpu.VMEM((9, COLS, BLOCK), F32),
-            pltpu.SMEM((2 * WIDTH + GROUP,), jnp.int32),
+            pltpu.SMEM((2 * WIDTH + GROUPS[0],), jnp.int32),
         ],
     )(lists, density.T, marks)
     sides = gather(side, axis_index_groups=pair_groups(boxes))
@@ -305,15 +309,15 @@
             pltpu.VMEM((8, 8, 128), F32),
             pltpu.VMEM((8, 8, 128), F32),
             pltpu.VMEM((4, COLS, BLOCK), BF16),
-            pltpu.VMEM((GROUP, BLOCK, BLOCK), BF16),
+            pltpu.VMEM((GROUPS[1], BLOCK, BLOCK), BF16),
             pltpu.VMEM((5, COLS, BLOCK), F32),
-            pltpu.SMEM((4 * WIDTH + GROUP,), jnp.int32),
+            pltpu.SMEM((4 * WIDTH + GROUPS[1],), jnp.int32),
             pltpu.SemaphoreType.DMA,
         ],
     )(parts)
     sides = gather(side, axis_index_groups=pair_groups(boxes))
     came = jnp.where(ahead == 1, sides[1], sides[0])
-    both = gather(own + came.astype(F32), axis_index_groups=core_groups(boxes))
+    both = gather((own + came.astype(F32)).astype(BF16), axis_index_groups=core_groups(boxes))
     density_two = call(
         last_kernel,
         "last",

time: 45.3 us -> 44.5 us (0.982)
  blocking collectives: 39.6 us -> 39.1 us
  Pallas kernels: 4.05 us -> 3.59 us
    pallas_call x1, Pallas kernels: 1.48 us -> 1 us  [body(): call(second_kernel, 'second', (shaped(COLS, rows, dtype=BF16), shaped(2 *...]
where the time goes in v5:
time: 44.5 us; the launch traced here: 44.3 us
  blocking collectives  39.1 us (88%)
  Pallas kernels  3.59 us (8%)
  between operations  0.8 us (2%)
  local copies, waits for them, and re-layouts  0.72 us (2%)
    all_gather x2, blocking collectives, body(): sides = gather(side, axis_index_groups=pair_groups(boxes))  16.4 us
    all_gather x1, blocking collectives, body(): lists = lax.all_gather(lists, 'seg')  11.9 us
    all_gather x1, blocking collectives, body(): gather(jnp.concatenate([mixed, meta], axis=0), axis_index_groups=half_gro...  8.86 us
    all_gather x1, blocking collectives, body(): gather((own + came.astype(F32)).astype(BF16), axis_index_groups=core_grou...  1.9 us
    pallas_call x1, Pallas kernels, body(): call(sort_kernel, 'sort', (shaped(48, 128, dtype=BF16), shaped(8, 128)),...  1.18 us
    pallas_call x1, Pallas kernels, body(): call(second_kernel, 'second', (shaped(COLS, rows, dtype=BF16), shaped(2 *...  1 us

profile of v5, /device:TPU:1, one launch (start us, length us, event | category | flops | bytes accessed | tf_op | source)
XLA Modules:
  0.0 44.3 jit_solution(8589801156748925501)
XLA Ops:
  0.7 0.0 copy-start.9
  0.7 0.0 copy-start.8
  0.7 0.0 copy-start.1
  0.7 0.0 copy-start.2
  0.7 0.0 copy-start.3
  0.8 0.0 copy-start
  0.8 0.6 %copy-done.9 = s32[2,4]{1,0:T(2,128)S(1)} copy-done((s32[2,4]{1,0:T(2,128)S(1)}, s32[2,4]{1,0:T(2,128)}, u32[]{:S(2)}) %copy-start.9) | copy-done | bytes 56
  1.3 0.0 copy-done.8
  1.4 0.0 copy-done.1
  1.4 0.0 copy-done.2
  1.4 0.0 copy-done.3
  1.4 0.0 copy-done.4
  1.4 0.0 copy-done.5
  1.4 0.0 copy-done.6
  1.5 0.0 copy-done.7
  1.5 1.2 %sort.1 = (bf16[48,128]{1,0:T(8,128)(2,1)S(1)}, f32[8,128]{1,0:T(8,128)S(1)}) custom-call(s32[8,128]{1,0:T(8,128)S(1)} %bitcast.18, s32[8,128]{1,0:T(8,128)S(1)} %bitcast.19, s32[8,128]{1,0:T(8,128)S(1)} %bitcast.20, f32[8,128]{1,0:T(8,128)S(1)} %bitcast.21, s32[8,128]{1,0:T(8,128)S(1)} %bitcast.22, s32[8,128]{1,0:T(8,128)S(1)} %bitcast.23, ...), custom_call_target="tpu_custom_call" | custom-call | tf_op jit(solution)/shard_map/sort/pallas_call | solution.py:276
  2.7 11.9 %all-gather = bf16[192,128]{1,0:T(8,128)(2,1)S(1)} all-gather(bf16[48,128]{1,0:T(8,128)(2,1)S(1)} %get-tuple-element.10), channel_id=2, replica_groups=mesh['box'=128,'seg'=4] {'seg'}, dimensions={0}, use_global_device_ids=true | all-gather | bytes 61440 | tf_op jit(solution)/shard_map/all_gather | solution.py:283
  14.6 0.7 %first.1 = (bf16[256,256]{1,0:T(8,128)(2,1)S(1)}, f32[256,256]{1,0:T(8,128)S(1)}, bf16[32,256]{1,0:T(8,128)(2,1)S(1)}) custom-call(bf16[4,48,128]{2,1,0:T(8,128)(2,1)S(1)} %bitcast.16, bf16[64,512]{1,0:T(8,128)(2,1)S(1)} %bitcast.17, f32[8,128]{1,0:T(8,128)S(1)} %get-tuple-element.11.marks_ref), custom_call_target="tpu_custom_call" | custom-call | tf_op jit(solution)/shard_map/first/pallas_call | solution.py:284
  15.4 9.3 %all-gather.1 = bf16[512,256]{1,0:T(8,128)(2,1)S(1)} all-gather(bf16[256,256]{1,0:T(8,128)(2,1)S(1)} %get-tuple-element.13), channel_id=3, replica_groups={{0,8},{2,10},{4,12},{6,14},{9,17},{11,19},{13,21},{15,23},{16,24},{18,2..., dimensions={0}, use_global_device_ids=true | all-gather | bytes 393216 | tf_op jit(solution)/shard_map/all_gather | solution.py:298
  24.7 8.9 %all-gather.2 = bf16[1152,256]{1,0:T(8,128)(2,1)S(1)} all-gather(bf16[288,256]{1,0:T(8,128)(2,1)S(1)} %pad_maximum_fusion), channel_id=4, replica_groups={{2,3,4,5},{0,1,6,7},{10,11,12,13},{8,9,14,15},{18,19,20,21},{16,17,22,2..., dimensions={0}, use_global_device_ids=true | all-gather | bytes 737280 | tf_op jit(solution)/shard_map/all_gather | solution.py:301
  33.6 1.0 %second.1 = (bf16[64,512]{1,0:T(8,128)(2,1)}, bf16[128,256]{1,0:T(8,128)(2,1)S(1)}, f32[128,256]{1,0:T(8,128)S(1)}) custom-call(bf16[4,288,256]{2,1,0:T(8,128)(2,1)S(1)} %bitcast.14), custom_call_target="tpu_custom_call" | custom-call | tf_op jit(solution)/shard_map/second/pallas_call | solution.py:302
  34.6 7.1 %all-gather.3 = bf16[256,256]{1,0:T(8,128)(2,1)S(1)} all-gather(bf16[128,256]{1,0:T(8,128)(2,1)S(1)} %get-tuple-element.17), channel_id=5, replica_groups={{0,8},{2,10},{4,12},{6,14},{9,17},{11,19},{13,21},{15,23},{16,24},{18,2..., dimensions={0}, use_global_device_ids=true | all-gather | bytes 196608 | tf_op jit(solution)/shard_map/all_gather | solution.py:318
  41.7 1.9 %all-gather.4 = bf16[256,256]{1,0:T(8,128)(2,1)S(1)} all-gather(bf16[128,256]{1,0:T(8,128)(2,1)S(1)} %fusion.1), channel_id=6, replica_groups={{0,1},{2,3},{4,5},{6,7},{8,9},{10,11},{12,13},{14,15},{16,17},{18,19},{..., dimensions={0}, use_global_device_ids=true | all-gather | bytes 196608 | tf_op jit(solution)/shard_map/all_gather | solution.py:320
  43.6 0.7 %last.1 = bf16[64,512]{1,0:T(8,128)(2,1)} custom-call(bf16[2,128,256]{2,1,0:T(8,128)(2,1)S(1)} %bitcast.15), custom_call_target="tpu_custom_call" | custom-call | tf_op jit(solution)/shard_map/last/pallas_call | solution.py:321
  (8 shorter events, 0.1 us)
Async XLA Ops:
  0.7 0.7 %copy-start.9 = (s32[2,4]{1,0:T(2,128)S(1)}, s32[2,4]{1,0:T(2,128)}, u32[]{:S(2)}) copy-start(s32[2,4]{1,0:T(2,128)} %refs_8_.1) | copy-start | bytes 100
  0.7 0.7 %copy-start.8 = (f32[1,1,1024]{2,1,0:T(1,128)S(1)}, f32[1,1,1024]{2,1,0:T(1,128)}, u32[]{:S(2)}) copy-start(f32[1,1,1024]{2,1,0:T(1,128)} %param.19) | copy-start | bytes 12292
  0.7 0.7 %copy-start.1 = (s32[1,1,1024]{2,1,0:T(1,128)S(1)}, s32[1,1,1024]{2,1,0:T(1,128)}, u32[]{:S(2)}) copy-start(s32[1,1,1024]{2,1,0:T(1,128)} %param.12) | copy-start | bytes 12292
  0.7 0.7 %copy-start.2 = (s32[1,1,1024]{2,1,0:T(1,128)S(1)}, s32[1,1,1024]{2,1,0:T(1,128)}, u32[]{:S(2)}) copy-start(s32[1,1,1024]{2,1,0:T(1,128)} %param.13) | copy-start | bytes 12292
  0.7 0.7 %copy-start.3 = (s32[1,1,1024]{2,1,0:T(1,128)S(1)}, s32[1,1,1024]{2,1,0:T(1,128)}, u32[]{:S(2)}) copy-start(s32[1,1,1024]{2,1,0:T(1,128)} %param.14) | copy-start | bytes 12292
  0.7 0.7 %copy-start.4 = (f32[1,1,1024]{2,1,0:T(1,128)S(1)}, f32[1,1,1024]{2,1,0:T(1,128)}, u32[]{:S(2)}) copy-start(f32[1,1,1024]{2,1,0:T(1,128)} %param.15) | copy-start | bytes 12292
  0.7 0.7 %copy-start.5 = (s32[1,1,1024]{2,1,0:T(1,128)S(1)}, s32[1,1,1024]{2,1,0:T(1,128)}, u32[]{:S(2)}) copy-start(s32[1,1,1024]{2,1,0:T(1,128)} %param.16) | copy-start | bytes 12292
  0.7 0.7 %copy-start.6 = (s32[1,1,1024]{2,1,0:T(1,128)S(1)}, s32[1,1,1024]{2,1,0:T(1,128)}, u32[]{:S(2)}) copy-start(s32[1,1,1024]{2,1,0:T(1,128)} %param.17) | copy-start | bytes 12292
  0.7 0.7 %copy-start.7 = (s32[1,1,1024]{2,1,0:T(1,128)S(1)}, s32[1,1,1024]{2,1,0:T(1,128)}, u32[]{:S(2)}) copy-start(s32[1,1,1024]{2,1,0:T(1,128)} %param.18) | copy-start | bytes 12292
  0.8 13.8 %copy-start = (bf16[512,64]{0,1:T(8,128)(2,1)S(1)}, bf16[512,64]{0,1:T(8,128)(2,1)}, u32[]{:S(2)}) copy-start(bf16[512,64]{0,1:T(8,128)(2,1)} %param.10) | copy-start | bytes 196612

commit v6 on v4

--- a/solution.py
+++ b/solution.py
@@ -235,7 +235,7 @@
 
 
 def last_kernel(both_ref, density_ref, stage_ref, sem):
-    total = (both_ref[0] + both_ref[1]).astype(BF16)
+    total = (both_ref[0].astype(F32) + both_ref[1].astype(F32)).astype(BF16)
     stage_ref[:, :BLOCK] = total[:COLS]
     stage_ref[:, BLOCK:] = total[COLS:]
     store = pltpu.make_async_copy(stage_ref, density_ref, sem)
@@ -313,7 +313,7 @@
     )(parts)
     sides = gather(side, axis_index_groups=pair_groups(boxes))
     came = jnp.where(ahead == 1, sides[1], sides[0])
-    both = gather(own + came.astype(F32), axis_index_groups=core_groups(boxes))
+    both = gather((own + came.astype(F32)).astype(BF16), axis_index_groups=core_groups(boxes))
     density_two = call(
         last_kernel,
         "last",

time: 45.3 us -> 44.4 us (0.980)
  Pallas kernels: 4.05 us -> 3.49 us
  blocking collectives: 39.6 us -> 39.1 us
    pallas_call x1, Pallas kernels: 1.48 us -> 0.91 us  [body(): call(second_kernel, 'second', (shaped(COLS, rows, dtype=BF16), shaped(2 *...]
where the time goes in v6:
time: 44.4 us; the launch traced here: 44.2 us
  blocking collectives  39.1 us (88%)
  Pallas kernels  3.49 us (8%)
  between operations  0.8 us (2%)
  local copies, waits for them, and re-layouts  0.72 us (2%)
    all_gather x2, blocking collectives, body(): sides = gather(side, axis_index_groups=pair_groups(boxes))  16.4 us
    all_gather x1, blocking collectives, body(): lists = lax.all_gather(lists, 'seg')  12 us
    all_gather x1, blocking collectives, body(): gather(jnp.concatenate([mixed, meta], axis=0), axis_index_groups=half_gro...  8.86 us
    all_gather x1, blocking collectives, body(): gather((own + came.astype(F32)).astype(BF16), axis_index_groups=core_grou...  1.9 us
    pallas_call x1, Pallas kernels, body(): call(sort_kernel, 'sort', (shaped(32, 128), shaped(8, 128)), (VMEM, VMEM)...  1.18 us
    pallas_call x1, Pallas kernels, body(): call(second_kernel, 'second', (shaped(COLS, rows, dtype=BF16), shaped(2 *...  0.91 us

profile of v6, /device:TPU:1, one launch (start us, length us, event | category | flops | bytes accessed | tf_op | source)
XLA Modules:
  0.0 44.2 jit_solution(12088035187855702132)
XLA Ops:
  0.7 0.0 copy-start.9
  0.7 0.0 copy-start.8
  0.7 0.0 copy-start.7
  0.7 0.0 copy-start.6
  0.7 0.0 copy-start.5
  0.8 0.6 %copy-done.9 = s32[2,4]{1,0:T(2,128)S(1)} copy-done((s32[2,4]{1,0:T(2,128)S(1)}, s32[2,4]{1,0:T(2,128)}, u32[]{:S(2)}) %copy-start.9) | copy-done | bytes 56
  1.3 0.0 copy-done.8
  1.4 0.0 copy-done.7
  1.4 0.0 copy-done.6
  1.4 0.0 copy-done.5
  1.4 0.0 copy-done.4
  1.4 0.0 copy-done.3
  1.4 0.0 copy-done.1
  1.5 0.0 copy-done.2
  1.5 1.2 %sort.1 = (f32[32,128]{1,0:T(8,128)S(1)}, f32[8,128]{1,0:T(8,128)S(1)}) custom-call(s32[8,128]{1,0:T(8,128)S(1)} %bitcast.18, s32[8,128]{1,0:T(8,128)S(1)} %bitcast.19, s32[8,128]{1,0:T(8,128)S(1)} %bitcast.20, f32[8,128]{1,0:T(8,128)S(1)} %bitcast.21, s32[8,128]{1,0:T(8,128)S(1)} %bitcast.22, s32[8,128]{1,0:T(8,128)S(1)} %bitcast.23, ...), custom_call_target="tpu_custom_call" | custom-call | tf_op jit(solution)/shard_map/sort/pallas_call | solution.py:272
  2.7 12.0 %all-gather = f32[128,128]{1,0:T(8,128)S(1)} all-gather(f32[32,128]{1,0:T(8,128)S(1)} %get-tuple-element.10), channel_id=2, replica_groups=mesh['box'=128,'seg'=4] {'seg'}, dimensions={0}, use_global_device_ids=true | all-gather | bytes 81920 | tf_op jit(solution)/shard_map/all_gather | solution.py:279
  14.6 0.0 copy-done
  14.6 0.7 %first.1 = (bf16[256,256]{1,0:T(8,128)(2,1)S(1)}, f32[256,256]{1,0:T(8,128)S(1)}, bf16[32,256]{1,0:T(8,128)(2,1)S(1)}) custom-call(f32[4,32,128]{2,1,0:T(8,128)S(1)} %bitcast.16, bf16[64,512]{1,0:T(8,128)(2,1)S(1)} %bitcast.17, f32[8,128]{1,0:T(8,128)S(1)} %get-tuple-element.11.marks_ref), custom_call_target="tpu_custom_call" | custom-call | tf_op jit(solution)/shard_map/first/pallas_call | solution.py:280
  15.4 9.3 %all-gather.1 = bf16[512,256]{1,0:T(8,128)(2,1)S(1)} all-gather(bf16[256,256]{1,0:T(8,128)(2,1)S(1)} %get-tuple-element.13), channel_id=3, replica_groups={{0,8},{2,10},{4,12},{6,14},{9,17},{11,19},{13,21},{15,23},{16,24},{18,2..., dimensions={0}, use_global_device_ids=true | all-gather | bytes 393216 | tf_op jit(solution)/shard_map/all_gather | solution.py:294
  24.7 8.9 %all-gather.2 = bf16[1152,256]{1,0:T(8,128)(2,1)S(1)} all-gather(bf16[288,256]{1,0:T(8,128)(2,1)S(1)} %pad_maximum_fusion), channel_id=4, replica_groups={{2,3,4,5},{0,1,6,7},{10,11,12,13},{8,9,14,15},{18,19,20,21},{16,17,22,2..., dimensions={0}, use_global_device_ids=true | all-gather | bytes 737280 | tf_op jit(solution)/shard_map/all_gather | solution.py:297
  33.6 0.9 %second.1 = (bf16[64,512]{1,0:T(8,128)(2,1)}, bf16[128,256]{1,0:T(8,128)(2,1)S(1)}, f32[128,256]{1,0:T(8,128)S(1)}) custom-call(bf16[4,288,256]{2,1,0:T(8,128)(2,1)S(1)} %bitcast.14), custom_call_target="tpu_custom_call" | custom-call | tf_op jit(solution)/shard_map/second/pallas_call | solution.py:298
  34.5 7.1 %all-gather.3 = bf16[256,256]{1,0:T(8,128)(2,1)S(1)} all-gather(bf16[128,256]{1,0:T(8,128)(2,1)S(1)} %get-tuple-element.17), channel_id=5, replica_groups={{0,8},{2,10},{4,12},{6,14},{9,17},{11,19},{13,21},{15,23},{16,24},{18,2..., dimensions={0}, use_global_device_ids=true | all-gather | bytes 196608 | tf_op jit(solution)/shard_map/all_gather | solution.py:314
  41.7 1.9 %all-gather.4 = bf16[256,256]{1,0:T(8,128)(2,1)S(1)} all-gather(bf16[128,256]{1,0:T(8,128)(2,1)S(1)} %fusion.1), channel_id=6, replica_groups={{0,1},{2,3},{4,5},{6,7},{8,9},{10,11},{12,13},{14,15},{16,17},{18,19},{..., dimensions={0}, use_global_device_ids=true | all-gather | bytes 196608 | tf_op jit(solution)/shard_map/all_gather | solution.py:316
  43.6 0.7 %last.1 = bf16[64,512]{1,0:T(8,128)(2,1)} custom-call(bf16[2,128,256]{2,1,0:T(8,128)(2,1)S(1)} %bitcast.15), custom_call_target="tpu_custom_call" | custom-call | tf_op jit(solution)/shard_map/last/pallas_call | solution.py:317
  (8 shorter events, 0.1 us)
Async XLA Ops:
  0.7 0.7 %copy-start.9 = (s32[2,4]{1,0:T(2,128)S(1)}, s32[2,4]{1,0:T(2,128)}, u32[]{:S(2)}) copy-start(s32[2,4]{1,0:T(2,128)} %refs_8_.1) | copy-start | bytes 100
  0.7 0.7 %copy-start.8 = (f32[1,1,1024]{2,1,0:T(1,128)S(1)}, f32[1,1,1024]{2,1,0:T(1,128)}, u32[]{:S(2)}) copy-start(f32[1,1,1024]{2,1,0:T(1,128)} %param.19) | copy-start | bytes 12292
  0.7 0.7 %copy-start.7 = (s32[1,1,1024]{2,1,0:T(1,128)S(1)}, s32[1,1,1024]{2,1,0:T(1,128)}, u32[]{:S(2)}) copy-start(s32[1,1,1024]{2,1,0:T(1,128)} %param.18) | copy-start | bytes 12292
  0.7 0.7 %copy-start.6 = (s32[1,1,1024]{2,1,0:T(1,128)S(1)}, s32[1,1,1024]{2,1,0:T(1,128)}, u32[]{:S(2)}) copy-start(s32[1,1,1024]{2,1,0:T(1,128)} %param.17) | copy-start | bytes 12292
  0.7 0.7 %copy-start.5 = (s32[1,1,1024]{2,1,0:T(1,128)S(1)}, s32[1,1,1024]{2,1,0:T(1,128)}, u32[]{:S(2)}) copy-start(s32[1,1,1024]{2,1,0:T(1,128)} %param.16) | copy-start | bytes 12292
  0.7 0.7 %copy-start.4 = (f32[1,1,1024]{2,1,0:T(1,128)S(1)}, f32[1,1,1024]{2,1,0:T(1,128)}, u32[]{:S(2)}) copy-start(f32[1,1,1024]{2,1,0:T(1,128)} %param.15) | copy-start | bytes 12292
  0.7 0.7 %copy-start.3 = (s32[1,1,1024]{2,1,0:T(1,128)S(1)}, s32[1,1,1024]{2,1,0:T(1,128)}, u32[]{:S(2)}) copy-start(s32[1,1,1024]{2,1,0:T(1,128)} %param.14) | copy-start | bytes 12292
  0.7 0.7 %copy-start.1 = (s32[1,1,1024]{2,1,0:T(1,128)S(1)}, s32[1,1,1024]{2,1,0:T(1,128)}, u32[]{:S(2)}) copy-start(s32[1,1,1024]{2,1,0:T(1,128)} %param.12) | copy-start | bytes 12292
  0.8 0.7 %copy-start.2 = (s32[1,1,1024]{2,1,0:T(1,128)S(1)}, s32[1,1,1024]{2,1,0:T(1,128)}, u32[]{:S(2)}) copy-start(s32[1,1,1024]{2,1,0:T(1,128)} %param.13) | copy-start | bytes 12292
  0.8 13.9 %copy-start = (bf16[512,64]{0,1:T(8,128)(2,1)S(1)}, bf16[512,64]{0,1:T(8,128)(2,1)}, u32[]{:S(2)}) copy-start(bf16[512,64]{0,1:T(8,128)(2,1)} %param.10) | copy-start | bytes 196612
